TPU v7x, 256 devices: a whole 4x4x8 slice. The times are simulated.
256 devices in a mesh: tile: 16 (over z_hi, y), pulse: 16 (over x, z_lo, core).
Axes of the slice: x: 4, y: 4, z: 8 (z_hi: 4, z_lo: 2; z = z_hi * 2 + z_lo), core: 2. Of those that a mesh axis runs over, the one named last changes fastest.
Arguments:
- profile: float32 [2, 128, 16384], P(None, 'pulse', 'tile'), may hold values from -6 to 6
- base_bin: int32 [128, 65536], P('pulse', 'tile'), may hold values from 0 to 16376, as said below
- tap_offset: int32 [128, 65536], P('pulse', 'tile'), may hold values from 0 to 15
Outputs:
- image: float32 [2, 65536], P(None, ('tile', 'pulse'))
Inputs may be any that keep to these rules, and one draw needn't show every extreme that they name: `base_bin`: for each pulse and each aligned block of 256 pixels, the base bins lie within 505 consecutive bins, and in every block they span exactly that many.
All inputs are finite; a program needn't handle non-finite values.
Results may differ from a plain program's by a relative error of at most 0.0003.
Values sent between devices are 32-bit elements; how exact they have to be, the bound alone decides.
No kernel may reach another device: no remote copies, remote signals or barrier semaphores. Data moves between devices by JAX's collectives and lax.ppermute only.
A program may use at most 256 MiB of HBM per device.

v0:
```python
import math

import jax
import jax.numpy as jnp
from jax import lax
from jax.sharding import PartitionSpec as P

TAPS = 8
FRAC = 16
WINDOW = 512
BLOCK = 256


def tap_table():
    frac_part = jnp.arange(FRAC, dtype=jnp.float32)[:, None] / FRAC
    shift = jnp.arange(TAPS, dtype=jnp.float32)[None, :] - (TAPS // 2 - 1)
    offset = shift - frac_part
    values = jnp.sinc(offset) * (0.5 + 0.5 * jnp.cos(math.pi * offset / (TAPS // 2)))
    return values / jnp.sum(values, axis=1, keepdims=True)


def phase_angle(bins, offsets):
    fine = bins * FRAC + offsets
    steps = fine * 2861 % 4096
    return steps.astype(jnp.float32) * (2.0 * math.pi / 4096.0)


def backproject(whole, bins_all, offsets_all, table):
    pulse_count = bins_all.shape[0]
    pixel_count = bins_all.shape[1]
    bin_count = whole.shape[2]
    block_count = pixel_count // BLOCK
    positions = jnp.arange(WINDOW, dtype=jnp.int32)
    places = positions[None, :, None]
    levels = jnp.arange(FRAC, dtype=jnp.int32)[None, :]
    total = jnp.zeros((2, pixel_count), jnp.float32)
    for pulse_index in range(pulse_count):
        trace = whole[:, pulse_index, :]
        bins = bins_all[pulse_index].reshape(block_count, BLOCK)
        offsets = offsets_all[pulse_index]
        starts = jnp.minimum(jnp.min(bins, axis=1), bin_count - WINDOW)
        indices = starts[:, None] + positions[None, :]
        slabs = jnp.take(trace, indices, axis=1)
        selector = (levels == offsets[:, None]).astype(jnp.float32)
        weights = jnp.dot(
            selector, table, precision=lax.Precision.HIGHEST, preferred_element_type=jnp.float32
        )
        weights = weights.reshape(block_count, BLOCK, TAPS)
        distance = places - (bins - starts[:, None])[:, None, :]
        banded = jnp.zeros((block_count, WINDOW, BLOCK), jnp.float32)
        for shift in range(TAPS):
            banded = banded + jnp.where(distance == shift, weights[:, None, :, shift], 0.0)
        interp = jnp.einsum("cnw,nwb->cnb", slabs, banded, precision=lax.Precision.HIGHEST)
        interp = interp.reshape(2, pixel_count)
        angle = phase_angle(bins_all[pulse_index], offsets)
        cosine = jnp.cos(angle)
        sine = jnp.sin(angle)
        real_part = interp[0] * cosine - interp[1] * sine
        imag_part = interp[0] * sine + interp[1] * cosine
        total = total + jnp.stack([real_part, imag_part])
    return total


def local(profile, base_bin, tap_offset):
    pulse_count = base_bin.shape[0]
    scale = 1.0 / math.sqrt(pulse_count * lax.axis_size("pulse"))
    table = tap_table()
    whole = lax.all_gather(profile, "tile", axis=2, tiled=True)
    partial_value = backproject(whole, base_bin, tap_offset, table)
    image = lax.psum_scatter(partial_value, "pulse", scatter_dimension=1, tiled=True)
    return image * scale


def solution(mesh):
    return jax.shard_map(
        local,
        mesh=mesh,
        in_specs=(P(None, "pulse", "tile"), P("pulse", "tile"), P("pulse", "tile")),
        out_specs=P(None, ("tile", "pulse")),
        check_vma=False,
    )
```

profile of v0, /device:TPU:1, one launch (start us, length us, event | category | flops | bytes accessed | tf_op | source)
XLA Modules:
  0.0 1221.0 jit_solution(8083134268148683660)
XLA Ops:
  6.5 3.5 copy.85
  10.1 0.3 slice_reduce_fusion.7
  12.9 0.7 broadcast_subtract_fusion.6
  13.6 0.7 fusion.502
  14.4 0.7 broadcast_subtract_fusion.7
  15.4 0.3 fusion.431
  15.8 0.3 fusion.430
  16.3 0.3 fusion.429
  16.7 0.3 fusion.428
  17.2 0.3 fusion.427
  17.6 0.3 fusion.426
  18.1 0.3 fusion.425
  18.5 0.6 broadcast_clamp_fusion.6
  19.1 0.3 fusion.424
  19.5 0.6 broadcast_clamp_fusion.7
  20.4 0.6 copy_bitcast_fusion.48
  21.1 0.6 copy_bitcast_fusion.50
  21.7 0.6 copy_bitcast_fusion.52
  22.3 0.6 copy_bitcast_fusion.54
  22.9 0.7 fusion.501
  23.6 0.6 copy_bitcast_fusion.56
  24.2 0.6 copy_bitcast_fusion.58
  24.8 0.6 copy_bitcast_fusion.60
  25.4 0.6 copy_bitcast_fusion.62
  26.0 5.1 fusion.737
  31.1 700.1 %all-gather.2.cloned.1.call-done = f32[2,8,16384]{0,2,1:T(8,128)} async-done(((f32[2,8,1024]{0,2,1:T(8,128)}), f32[2,8,16384]{0,2,1:T(8,128)}) %all-gather.2.cloned.1.call-update) | async-done | bytes 1048592 | tf_op jit(solution)/shard_map/all_gather | solution.py:68
  731.2 44.5 %slice_bitcast_fusion.7 = (f32[2,16384]{0,1:T(8,128)}, f32[2,16384]{0,1:T(8,128)}, f32[2,16384]{0,1:T(8,128)}, f32[2,16384]{0,1:T(8,128)}, f32[2,16384]{0,1:T(8,...) fusion(f32[2,8,16384]{0,2,1:T(8,128)} %all-gather.2.cloned.1.call-done), kind=kLoop, calls=%fused_computation.15 | loop fusion | bytes 2097152 | tf_op jit(solution)/shard_map/squeeze | solution.py:38
  775.7 31.2 %gather_fusion.7 = f32[8192,2]{1,0:T(8,128)} fusion(f32[2,16384]{0,1:T(8,128)} %get-tuple-element.31, s32[8192]{0:T(1024)S(1)} %broadcast_clamp_fusion), kind=kCustom, calls=%fused_computation.7.clone | custom fusion | bytes 163840 | tf_op jit(solution)/shard_map/jit(_take)/gather | solution.py:43
  807.0 2.8 copy.93
  809.8 11.7 fusion.421
  821.5 31.2 %gather_fusion.6 = f32[8192,2]{1,0:T(8,128)} fusion(f32[2,16384]{0,1:T(8,128)} %get-tuple-element.32, s32[8192]{0:T(1024)S(1)} %broadcast_clamp_fusion.1), kind=kCustom, calls=%fused_computation.6.clone | custom fusion | bytes 163840 | tf_op jit(solution)/shard_map/jit(_take)/gather | solution.py:43
  852.8 2.8 copy.92
  855.6 11.7 fusion.418
  867.3 31.2 %gather_fusion.5 = f32[8192,2]{1,0:T(8,128)} fusion(f32[2,16384]{0,1:T(8,128)} %get-tuple-element.33, s32[8192]{0:T(1024)S(1)} %broadcast_clamp_fusion.2), kind=kCustom, calls=%fused_computation.5.clone | custom fusion | bytes 163840 | tf_op jit(solution)/shard_map/jit(_take)/gather | solution.py:43
  898.6 2.8 copy.91
  901.4 12.2 fusion.415
  913.7 31.2 %gather_fusion.4 = f32[8192,2]{1,0:T(8,128)} fusion(f32[2,16384]{0,1:T(8,128)} %get-tuple-element.34, s32[8192]{0:T(1024)S(1)} %broadcast_clamp_fusion.3), kind=kCustom, calls=%fused_computation.4.clone | custom fusion | bytes 163840 | tf_op jit(solution)/shard_map/jit(_take)/gather | solution.py:43
  944.9 2.8 copy.90
  947.7 11.7 fusion.412
  959.5 31.2 %gather_fusion.3 = f32[8192,2]{1,0:T(8,128)} fusion(f32[2,16384]{0,1:T(8,128)} %get-tuple-element.35, s32[8192]{0:T(1024)S(1)} %broadcast_clamp_fusion.4), kind=kCustom, calls=%fused_computation.3.clone | custom fusion | bytes 163840 | tf_op jit(solution)/shard_map/jit(_take)/gather | solution.py:43
  990.7 2.8 copy.89
  993.6 11.7 fusion.409
  1005.3 31.2 %gather_fusion.2 = f32[8192,2]{1,0:T(8,128)} fusion(f32[2,16384]{0,1:T(8,128)} %get-tuple-element.36, s32[8192]{0:T(1024)S(1)} %broadcast_clamp_fusion.5), kind=kCustom, calls=%fused_computation.2.clone | custom fusion | bytes 163840 | tf_op jit(solution)/shard_map/jit(_take)/gather | solution.py:43
  1036.5 2.8 copy.88
  1039.5 11.9 fusion.406
  1051.4 31.2 %gather_fusion.1 = f32[8192,2]{1,0:T(8,128)} fusion(f32[2,16384]{0,1:T(8,128)} %get-tuple-element.37, s32[8192]{0:T(1024)S(1)} %copy-done.3), kind=kCustom, calls=%fused_computation.1.clone | custom fusion | bytes 163840 | tf_op jit(solution)/shard_map/jit(_take)/gather | solution.py:43
  1082.6 2.8 copy.87
  1085.7 11.7 fusion.403
  1097.4 31.2 %gather_fusion = f32[8192,2]{1,0:T(8,128)} fusion(f32[2,16384]{0,1:T(8,128)} %get-tuple-element.30, s32[8192]{0:T(1024)S(1)} %copy-done.2), kind=kCustom, calls=%fused_computation.clone | custom fusion | bytes 163840 | tf_op jit(solution)/shard_map/jit(_take)/gather | solution.py:43
  1128.6 2.8 copy.86
  1131.7 11.9 fusion.400
  1143.7 0.5 multiply_subtract_fusion
  1144.2 0.5 multiply_subtract_fusion.1
  1144.6 0.5 multiply_subtract_fusion.2
  1145.1 0.5 multiply_subtract_fusion.3
  1145.6 0.5 multiply_subtract_fusion.4
  1146.1 0.5 multiply_subtract_fusion.5
  1146.6 0.5 multiply_subtract_fusion.6
  1147.0 0.5 multiply_subtract_fusion.7
  1147.5 0.2 maximum_add_fusion.1
  1147.7 2.0 copy.94
  1149.7 62.6 %reduce-scatter.4.cloned.1.call-done = f32[256,2]{1,0:T(8,128)} async-done(((f32[4096,2]{1,0:T(8,128)}), f32[256,2]{1,0:T(8,128)}) %reduce-scatter.4.cloned.1.call-update) | async-done | bytes 2064
  1212.4 1.0 copy.95
  1213.3 0.6 broadcast_multiply_fusion
  (186 shorter events, 4.3 us)
Async XLA Ops:
  6.5 3.6 copy-start.1
  6.5 8.6 copy-start
  6.5 724.7 %all-gather.2.cloned.1.call-start = ((), (), s32[]{:S(2)}) async-start(), calls=%async_computation.1 | async-start | bytes 71303168 | tf_op jit(solution)/shard_map/all_gather | solution.py:68
  10.0 1202.3 %reduce-scatter.4.cloned.1.call-start = ((), (), s32[]{:S(2)}) async-start(), calls=%async_computation.2 | async-start | bytes 2228224
  1039.4 12.0 copy-start.3
  1039.4 46.1 %copy-start.21 = (s32[16,256]{1,0:T(8,128)S(1)}, s32[16,256]{1,0:T(8,128)}, u32[]{:S(2)}) copy-start(s32[16,256]{1,0:T(8,128)} %broadcast_subtract_fusion.6) | copy-start | bytes 49156
  1039.4 46.1 %copy-start.24 = (f32[16,256]{1,0:T(8,128)S(1)}, f32[16,256]{1,0:T(8,128)}, u32[]{:S(2)}) copy-start(f32[16,256]{1,0:T(8,128)} %get-tuple-element.164) | copy-start | bytes 49156
  1039.4 46.1 %copy-start.25 = (f32[16,256]{1,0:T(8,128)S(1)}, f32[16,256]{1,0:T(8,128)}, u32[]{:S(2)}) copy-start(f32[16,256]{1,0:T(8,128)} %get-tuple-element.165) | copy-start | bytes 49156
  1039.4 46.1 %copy-start.28 = (f32[16,256]{1,0:T(8,128)S(1)}, f32[16,256]{1,0:T(8,128)}, u32[]{:S(2)}) copy-start(f32[16,256]{1,0:T(8,128)} %get-tuple-element.166) | copy-start | bytes 49156
  1039.4 46.1 %copy-start.29 = (f32[16,256]{1,0:T(8,128)S(1)}, f32[16,256]{1,0:T(8,128)}, u32[]{:S(2)}) copy-start(f32[16,256]{1,0:T(8,128)} %get-tuple-element.167) | copy-start | bytes 49156
  1039.4 46.1 %copy-start.32 = (f32[16,256]{1,0:T(8,128)S(1)}, f32[16,256]{1,0:T(8,128)}, u32[]{:S(2)}) copy-start(f32[16,256]{1,0:T(8,128)} %get-tuple-element.168) | copy-start | bytes 49156
  1039.4 46.1 %copy-start.33 = (f32[16,256]{1,0:T(8,128)S(1)}, f32[16,256]{1,0:T(8,128)}, u32[]{:S(2)}) copy-start(f32[16,256]{1,0:T(8,128)} %get-tuple-element.169) | copy-start | bytes 49156
  1039.4 46.1 %copy-start.36 = (f32[16,256]{1,0:T(8,128)S(1)}, f32[16,256]{1,0:T(8,128)}, u32[]{:S(2)}) copy-start(f32[16,256]{1,0:T(8,128)} %get-tuple-element.170) | copy-start | bytes 49156
  1039.4 46.1 %copy-start.37 = (f32[16,256]{1,0:T(8,128)S(1)}, f32[16,256]{1,0:T(8,128)}, u32[]{:S(2)}) copy-start(f32[16,256]{1,0:T(8,128)} %get-tuple-element.171) | copy-start | bytes 49156
  1039.4 46.1 %copy-start.38 = (pred[16,512]{1,0:T(8,128)(4,1)S(1)}, pred[16,512]{1,0:T(8,128)(4,1)}, u32[]{:S(2)}) copy-start(pred[16,512]{1,0:T(8,128)(4,1)} %fusion.502) | copy-start | bytes 24580
  1085.5 11.8 copy-start.2
  1085.6 45.9 %copy-start.20 = (s32[16,256]{1,0:T(8,128)S(1)}, s32[16,256]{1,0:T(8,128)}, u32[]{:S(2)}) copy-start(s32[16,256]{1,0:T(8,128)} %broadcast_subtract_fusion.7) | copy-start | bytes 49156
  1085.6 45.9 %copy-start.22 = (f32[16,256]{1,0:T(8,128)S(1)}, f32[16,256]{1,0:T(8,128)}, u32[]{:S(2)}) copy-start(f32[16,256]{1,0:T(8,128)} %get-tuple-element.156) | copy-start | bytes 49156
  1085.6 45.9 %copy-start.23 = (f32[16,256]{1,0:T(8,128)S(1)}, f32[16,256]{1,0:T(8,128)}, u32[]{:S(2)}) copy-start(f32[16,256]{1,0:T(8,128)} %get-tuple-element.157) | copy-start | bytes 49156
  1085.6 45.9 %copy-start.26 = (f32[16,256]{1,0:T(8,128)S(1)}, f32[16,256]{1,0:T(8,128)}, u32[]{:S(2)}) copy-start(f32[16,256]{1,0:T(8,128)} %get-tuple-element.158) | copy-start | bytes 49156
  1085.6 45.9 %copy-start.27 = (f32[16,256]{1,0:T(8,128)S(1)}, f32[16,256]{1,0:T(8,128)}, u32[]{:S(2)}) copy-start(f32[16,256]{1,0:T(8,128)} %get-tuple-element.159) | copy-start | bytes 49156
  1085.6 45.9 %copy-start.30 = (f32[16,256]{1,0:T(8,128)S(1)}, f32[16,256]{1,0:T(8,128)}, u32[]{:S(2)}) copy-start(f32[16,256]{1,0:T(8,128)} %get-tuple-element.160) | copy-start | bytes 49156
  1085.6 45.9 %copy-start.31 = (f32[16,256]{1,0:T(8,128)S(1)}, f32[16,256]{1,0:T(8,128)}, u32[]{:S(2)}) copy-start(f32[16,256]{1,0:T(8,128)} %get-tuple-element.161) | copy-start | bytes 49156
  1085.6 45.9 %copy-start.34 = (f32[16,256]{1,0:T(8,128)S(1)}, f32[16,256]{1,0:T(8,128)}, u32[]{:S(2)}) copy-start(f32[16,256]{1,0:T(8,128)} %get-tuple-element.162) | copy-start | bytes 49156
  1085.6 45.9 %copy-start.35 = (f32[16,256]{1,0:T(8,128)S(1)}, f32[16,256]{1,0:T(8,128)}, u32[]{:S(2)}) copy-start(f32[16,256]{1,0:T(8,128)} %get-tuple-element.163) | copy-start | bytes 49156
  1085.6 45.9 %copy-start.39 = (pred[16,512]{1,0:T(8,128)(4,1)S(1)}, pred[16,512]{1,0:T(8,128)(4,1)}, u32[]{:S(2)}) copy-start(pred[16,512]{1,0:T(8,128)(4,1)} %fusion.501) | copy-start | bytes 24580
  1131.6 12.1 copy-start.18
  1131.6 12.1 copy-start.19
  1131.6 12.6 %copy-start.16 = (f32[1,4096]{1,0:T(1,128)S(1)}, f32[1,4096]{1,0:T(1,128)}, u32[]{:S(2)}) copy-start(f32[1,4096]{1,0:T(1,128)} %get-tuple-element.48) | copy-start | bytes 49156
  1131.6 12.6 %copy-start.17 = (f32[1,4096]{1,0:T(1,128)S(1)}, f32[1,4096]{1,0:T(1,128)}, u32[]{:S(2)}) copy-start(f32[1,4096]{1,0:T(1,128)} %get-tuple-element.49) | copy-start | bytes 49156
  1131.6 13.0 %copy-start.14 = (f32[1,4096]{1,0:T(1,128)S(1)}, f32[1,4096]{1,0:T(1,128)}, u32[]{:S(2)}) copy-start(f32[1,4096]{1,0:T(1,128)} %get-tuple-element.46) | copy-start | bytes 49156
  1131.6 13.0 %copy-start.15 = (f32[1,4096]{1,0:T(1,128)S(1)}, f32[1,4096]{1,0:T(1,128)}, u32[]{:S(2)}) copy-start(f32[1,4096]{1,0:T(1,128)} %get-tuple-element.47) | copy-start | bytes 49156
  1131.6 13.5 %copy-start.12 = (f32[1,4096]{1,0:T(1,128)S(1)}, f32[1,4096]{1,0:T(1,128)}, u32[]{:S(2)}) copy-start(f32[1,4096]{1,0:T(1,128)} %get-tuple-element.44) | copy-start | bytes 49156
  1131.6 13.5 %copy-start.13 = (f32[1,4096]{1,0:T(1,128)S(1)}, f32[1,4096]{1,0:T(1,128)}, u32[]{:S(2)}) copy-start(f32[1,4096]{1,0:T(1,128)} %get-tuple-element.45) | copy-start | bytes 49156
  1131.7 13.9 %copy-start.10 = (f32[1,4096]{1,0:T(1,128)S(1)}, f32[1,4096]{1,0:T(1,128)}, u32[]{:S(2)}) copy-start(f32[1,4096]{1,0:T(1,128)} %get-tuple-element.42) | copy-start | bytes 49156
  1131.7 13.9 %copy-start.11 = (f32[1,4096]{1,0:T(1,128)S(1)}, f32[1,4096]{1,0:T(1,128)}, u32[]{:S(2)}) copy-start(f32[1,4096]{1,0:T(1,128)} %get-tuple-element.43) | copy-start | bytes 49156
  1131.7 14.4 %copy-start.8 = (f32[1,4096]{1,0:T(1,128)S(1)}, f32[1,4096]{1,0:T(1,128)}, u32[]{:S(2)}) copy-start(f32[1,4096]{1,0:T(1,128)} %get-tuple-element.40) | copy-start | bytes 49156
  1131.7 14.4 %copy-start.9 = (f32[1,4096]{1,0:T(1,128)S(1)}, f32[1,4096]{1,0:T(1,128)}, u32[]{:S(2)}) copy-start(f32[1,4096]{1,0:T(1,128)} %get-tuple-element.41) | copy-start | bytes 49156
  1131.7 14.9 %copy-start.6 = (f32[1,4096]{1,0:T(1,128)S(1)}, f32[1,4096]{1,0:T(1,128)}, u32[]{:S(2)}) copy-start(f32[1,4096]{1,0:T(1,128)} %get-tuple-element.38) | copy-start | bytes 49156
  1131.7 14.9 %copy-start.7 = (f32[1,4096]{1,0:T(1,128)S(1)}, f32[1,4096]{1,0:T(1,128)}, u32[]{:S(2)}) copy-start(f32[1,4096]{1,0:T(1,128)} %get-tuple-element.39) | copy-start | bytes 49156
  1131.7 15.3 %copy-start.4 = (f32[1,4096]{1,0:T(1,128)S(1)}, f32[1,4096]{1,0:T(1,128)}, u32[]{:S(2)}) copy-start(f32[1,4096]{1,0:T(1,128)} %get-tuple-element.14) | copy-start | bytes 49156
  1131.7 15.3 %copy-start.5 = (f32[1,4096]{1,0:T(1,128)S(1)}, f32[1,4096]{1,0:T(1,128)}, u32[]{:S(2)}) copy-start(f32[1,4096]{1,0:T(1,128)} %get-tuple-element.15) | copy-start | bytes 49156
Sparse Core Ops, SparseCore 0:
  10.2 720.9 all-gather.1
  1149.9 62.4 reduce-scatter.3
where the time goes:
time: 1230 us; the launch traced here: 1220 us
  waiting for transfers between devices  763 us (62%)
  local copies, waits for them, and re-layouts  330 us (27%)
  matrix products  96.8 us (8%)
  other arithmetic  16.2 us (1%)
  between operations  14.9 us (1%)
    all_gather x1, waiting for transfers between devices, local(): whole = lax.all_gather(profile, 'tile', axis=2, tiled=True)  700 us
    gather x16, local copies, waits for them, and re-layouts, backproject(): slabs = jnp.take(trace, indices, axis=1)  273 us
    dot_general x8, matrix products, backproject(): jnp.einsum('cnw,nwb->cnb', slabs, banded, precision=lax.Precision.HIGHEST)  94.4 us
    unnamed x3, waiting for transfers between devices  62.6 us
    squeeze x1, local copies, waits for them, and re-layouts, backproject(): trace = whole[:, pulse_index, :]  44.5 us
  transfers between devices with their start and end apart: 2, of which 2 were waited for; matrix products, arithmetic and copies ran while one was open for 2% of the time, Pallas kernels for 0%

commit v1 on v0

v1 whole, which is shorter than its diff:
```python
import math

import jax
import jax.numpy as jnp
from jax import lax
from jax.experimental import pallas as pl
from jax.experimental.pallas import tpu as pltpu
from jax.sharding import PartitionSpec as P

TAPS = 8
FRAC = 16
BLOCK = 256
LANES = 128
REACH = 5
SIDE = 4


def tap_table():
    frac_part = jnp.arange(FRAC, dtype=jnp.float32)[:, None] / FRAC
    shift = jnp.arange(TAPS, dtype=jnp.float32)[None, :] - (TAPS // 2 - 1)
    offset = shift - frac_part
    values = jnp.sinc(offset) * (0.5 + 0.5 * jnp.cos(math.pi * offset / (TAPS // 2)))
    values = values / jnp.sum(values, axis=1, keepdims=True)
    return jnp.pad(values.T, ((0, 0), (0, LANES - FRAC)))


def lane_take(row, index):
    return jnp.take_along_axis(row, index, axis=1, mode="promise_in_bounds")


def cos_sin(steps):
    quarter = (steps + 512) >> 10
    x = (steps - (quarter << 10)).astype(jnp.float32) * (2.0 * math.pi / 4096.0)
    y = x * x
    s = x * (1.0 + y * (-1.0 / 6.0 + y * (1.0 / 120.0 + y * (-1.0 / 5040.0 + y * (1.0 / 362880.0)))))
    c = 1.0 + y * (-0.5 + y * (1.0 / 24.0 + y * (-1.0 / 720.0 + y * (1.0 / 40320.0))))
    odd = (quarter & 1) == 1
    cosine = jnp.where(odd, s, c)
    sine = jnp.where(odd, c, s)
    cosine = jnp.where(((quarter + 1) & 2) == 2, -cosine, cosine)
    sine = jnp.where((quarter & 2) == 2, -sine, sine)
    return cosine, sine


def prepare_kernel(table_ref, first_ref, bins_ref, offsets_ref, rel_ref, weight_ref, cos_ref, sin_ref):
    pixels = bins_ref.shape[1]
    tables = [jnp.broadcast_to(table_ref[j : j + 1, :], (8, LANES)) for j in range(TAPS)]
    for part in range(pixels // LANES):
        lanes = pl.ds(part * LANES, LANES)
        block = part * LANES // BLOCK
        bins = bins_ref[:, lanes]
        offsets = offsets_ref[:, lanes]
        rel_ref[:, lanes] = bins - first_ref[:, block : block + 1] * LANES
        steps = ((bins * FRAC + offsets) * 2861) & 4095
        cosine, sine = cos_sin(steps)
        cos_ref[:, lanes] = cosine
        sin_ref[:, lanes] = sine
        for j in range(TAPS):
            weight_ref[j, :, lanes] = lane_take(tables[j], offsets)


def project_kernel(scale, place_ref, first_ref, p0, p1, p2, p3, rel_ref, weight_ref, cos_ref, sin_ref, out_ref, whole, window):
    pulses, pixels = rel_ref.shape
    bins = p0.shape[3]
    my_z, my_y = place_ref[0], place_ref[1]
    for dy, piece in enumerate((p0, p1, p2, p3)):
        for dz in range(SIDE):
            owner = ((my_z - dz) & (SIDE - 1)) * SIDE + ((my_y - dy) & (SIDE - 1))
            for c in range(2):
                for t in range(bins // LANES):
                    whole[c, owner * (bins // LANES) + t] = piece[dz, c, :, t * LANES : (t + 1) * LANES]
    for block in range(pixels // BLOCK):
        for s in range(pulses):
            first = first_ref[s, block]
            for c in range(2):
                for r in range(REACH):
                    window[block, c, r, s : s + 1, :] = whole[c, first + r, s : s + 1, :]
    for block in range(pixels // BLOCK):
        for half in range(BLOCK // LANES):
            lanes = pl.ds(block * BLOCK + half * LANES, LANES)
            rel = rel_ref[:, lanes]
            real = jnp.zeros((pulses, LANES), jnp.float32)
            imag = jnp.zeros((pulses, LANES), jnp.float32)
            for j in range(TAPS):
                index = rel + j
                lane = index & (LANES - 1)
                row = index >> 7
                got = [lane_take(window[block, c, 0], lane) for c in range(2)]
                for r in range(1, REACH):
                    here = row == r
                    for c in range(2):
                        got[c] = jnp.where(here, lane_take(window[block, c, r], lane), got[c])
                weight = weight_ref[j, :, lanes]
                real = real + weight * got[0]
                imag = imag + weight * got[1]
            cosine = cos_ref[:, lanes]
            sine = sin_ref[:, lanes]
            out_ref[block, half : half + 1, :] = jnp.sum(real * cosine - imag * sine, axis=0, keepdims=True) * scale
            out_ref[block, 2 + half : 3 + half, :] = jnp.sum(real * sine + imag * cosine, axis=0, keepdims=True) * scale


def shifted(dz, dy):
    return [
        (z * SIDE + y, (z + dz) % SIDE * SIDE + (y + dy) % SIDE) for z in range(SIDE) for y in range(SIDE)
    ]


def local(profile, base_bin, tap_offset):
    pulses, pixels = base_bin.shape
    blocks = pixels // BLOCK
    bins = profile.shape[2]
    scale = 1.0 / math.sqrt(pulses * lax.axis_size("pulse"))
    me = lax.axis_index("tile")
    place = jnp.stack([me // SIDE, me % SIDE]).astype(jnp.int32)

    column = [profile] + [lax.ppermute(profile, "tile", shifted(dz, 0)) for dz in range(1, SIDE)]
    column = jnp.stack(column)
    pieces = [column] + [lax.ppermute(column, "tile", shifted(0, dy)) for dy in range(1, SIDE)]

    first = jnp.min(base_bin.reshape(pulses, blocks, BLOCK), axis=2) >> 7
    vmem = pl.BlockSpec(memory_space=pltpu.VMEM)
    smem = pl.BlockSpec(memory_space=pltpu.SMEM)
    rel, weight, cosine, sine = pl.pallas_call(
        prepare_kernel,
        out_shape=[
            jax.ShapeDtypeStruct((pulses, pixels), jnp.int32),
            jax.ShapeDtypeStruct((TAPS, pulses, pixels), jnp.float32),
            jax.ShapeDtypeStruct((pulses, pixels), jnp.float32),
            jax.ShapeDtypeStruct((pulses, pixels), jnp.float32),
        ],
        in_specs=[vmem] * 4,
        out_specs=[vmem] * 4,
        cost_estimate=pl.CostEstimate(flops=pulses * pixels * 300, bytes_accessed=pulses * pixels * 52, transcendentals=0),
        compiler_params=pltpu.CompilerParams(vmem_limit_bytes=16 << 20),
        name="prepare",
    )(tap_table(), first, base_bin, tap_offset)
    partial_image = pl.pallas_call(
        lambda *refs: project_kernel(scale, *refs),
        out_shape=jax.ShapeDtypeStruct((blocks, 4, LANES), jnp.float32),
        in_specs=[smem] * 2 + [vmem] * 8,
        out_specs=vmem,
        scratch_shapes=[
            pltpu.VMEM((2, SIDE * SIDE * bins // LANES + REACH, pulses, LANES), jnp.float32),
            pltpu.VMEM((blocks, 2, REACH, pulses, LANES), jnp.float32),
        ],
        compiler_params=pltpu.CompilerParams(vmem_limit_bytes=32 << 20),
        name="project",
    )(place, first, *pieces, rel, weight, cosine, sine)
    parts = lax.all_to_all(partial_image, "pulse", 0, 0, tiled=True)
    return jnp.sum(parts, axis=0).reshape(2, BLOCK)


def solution(mesh):
    return jax.shard_map(
        local,
        mesh=mesh,
        in_specs=(P(None, "pulse", "tile"), P("pulse", "tile"), P("pulse", "tile")),
        out_specs=P(None, ("tile", "pulse")),
        check_vma=False,
    )
```

time: 1230 us -> 50.9 us (0.04)
  waiting for transfers between devices: 763 us -> 13.9 us
  local copies, waits for them, and re-layouts: 330 us -> 0.68 us
  matrix products: 96.8 us -> 0 us
  starting transfers between devices: 0.04 us -> 15.2 us
  between operations: 14.9 us -> 0.07 us
  other arithmetic: 16.2 us -> 1.66 us
  blocking collectives: 0 us -> 14.3 us
    all_gather x1 -> x0, waiting for transfers between devices: 700 us -> none  [local(): whole = lax.all_gather(profile, 'tile', axis=2, tiled=True)]
    gather x16 -> x0, local copies, waits for them, and re-layouts: 273 us -> none  [backproject(): slabs = jnp.take(trace, indices, axis=1)]
    dot_general x16 -> x0, matrix products: 96.8 us -> none  [the longest x8 94.4 us: backproject(): jnp.einsum('cnw,nwb->cnb', slabs, banded, precision=lax.Precision.HIGHEST)]
    unnamed x3 -> x0, waiting for transfers between devices: 62.6 us -> none
    squeeze x1 -> x0, local copies, waits for them, and re-layouts: 44.5 us -> none  [backproject(): trace = whole[:, pulse_index, :]]
    ppermute x0 -> x6, starting transfers between devices: none -> 15.2 us  [the longest x3 11.3 us: local(): lax.ppermute(profile, 'tile', shifted(dz, 0))]
    all_to_all x0 -> x1, blocking collectives: none -> 14.3 us  [local(): parts = lax.all_to_all(partial_image, 'pulse', 0, 0, tiled=True)]
    ppermute x0 -> x6, waiting for transfers between devices: none -> 13.9 us  [the longest x3 12.7 us: local(): lax.ppermute(column, 'tile', shifted(0, dy))]
  transfers between devices with their start and end apart: 2 -> 6, of which waited for: 2 -> 4; matrix products, arithmetic and copies ran while one was open for 2% -> 3% of each run, Pallas kernels for 0% -> 1%
where the time goes in v1:
time: 50.9 us; the launch traced here: 50.7 us
  starting transfers between devices  15.2 us (30%)
  blocking collectives  14.3 us (28%)
  waiting for transfers between devices  13.9 us (27%)
  Pallas kernels  4.99 us (10%)
  other arithmetic  1.66 us (3%)
  local copies, waits for them, and re-layouts  0.68 us (1%)
    all_to_all x1, blocking collectives, local(): parts = lax.all_to_all(partial_image, 'pulse', 0, 0, tiled=True)  14.3 us
    ppermute x3, waiting for transfers between devices, local(): lax.ppermute(column, 'tile', shifted(0, dy))  12.7 us
    ppermute x3, starting transfers between devices, local(): lax.ppermute(profile, 'tile', shifted(dz, 0))  11.3 us
    pallas_call x1, Pallas kernels, local(): pl.pallas_call(lambda *refs: project_kernel(scale, *refs), out_shape=jax....  4.51 us
    ppermute x3, starting transfers between devices, local(): lax.ppermute(column, 'tile', shifted(0, dy))  3.85 us
    reduce_min x1, other arithmetic, local(): first = jnp.min(base_bin.reshape(pulses, blocks, BLOCK), axis=2) >> 7  1.28 us
    ppermute x3, waiting for transfers between devices, local(): lax.ppermute(profile, 'tile', shifted(dz, 0))  1.13 us
  transfers between devices with their start and end apart: 6, of which 4 were waited for; matrix products, arithmetic and copies ran while one was open for 3% of the time, Pallas kernels for 1%

profile of v1, /device:TPU:1, one launch (start us, length us, event | category | flops | bytes accessed | tf_op | source)
XLA Modules:
  0.0 50.7 jit_solution(17767008914140020072)
XLA Ops:
  0.0 3.8 %collective-permute-start = (f32[2,8,1024]{2,1,0:T(8,128)}, f32[2,8,1024]{2,1,0:T(8,128)S(1)}, u32[]{:S(2)}, u32[]{:S(2)}) collective-permute-start(f32[2,8,1024]{2,1,0:T(8,128)} %param.3), channel_id=1, source_target_pairs={{0,64},{16,80},{32,96},{48,112},{64,128},{80,144},{96,160},{112,17... | collective-permute-start | bytes 196616 | tf_op jit(solution)/shard_map/ppermute | solution.py:116
  3.8 3.0 %collective-permute-start.2 = (f32[2,8,1024]{2,1,0:T(8,128)}, f32[2,8,1024]{2,1,0:T(8,128)S(1)}, u32[]{:S(2)}, u32[]{:S(2)}) collective-permute-start(f32[2,8,1024]{2,1,0:T(8,128)} %param.3), channel_id=1, source_target_pairs={{0,192},{16,208},{32,224},{48,240},{64,0},{80,16},{96,32},{112,48}... | collective-permute-start | bytes 196616 | tf_op jit(solution)/shard_map/ppermute | solution.py:116
  6.9 4.5 %collective-permute-start.1 = (f32[2,8,1024]{2,1,0:T(8,128)}, f32[2,8,1024]{2,1,0:T(8,128)S(1)}, u32[]{:S(2)}, u32[]{:S(2)}) collective-permute-start(f32[2,8,1024]{2,1,0:T(8,128)} %param.3), channel_id=1, source_target_pairs={{0,128},{16,144},{32,160},{48,176},{64,192},{80,208},{96,224},{112... | collective-permute-start | bytes 196616 | tf_op jit(solution)/shard_map/ppermute | solution.py:116
  11.3 0.1 fusion.55
  11.5 0.1 fusion.9
  11.6 0.0 copy-start.2
  11.6 1.3 %reduce_min.9 = s32[8,16]{0,1:T(8,128)S(1)} reduce(s32[8,16,256]{2,0,1:T(8,128)} %bitcast.7, s32[]{:T(128)} %constant.73.clone.1), dimensions={2}, to_apply=%region_0.1 | reduce | flops 32640 | bytes 131588 | tf_op jit(solution)/shard_map/reduce_min | solution.py:120
  12.9 0.1 copy.5
  13.0 0.0 collective-permute-done
  13.0 0.0 collective-permute-done.2
  13.0 1.1 %collective-permute-done.1 = f32[2,8,1024]{2,1,0:T(8,128)S(1)} collective-permute-done((f32[2,8,1024]{2,1,0:T(8,128)}, f32[2,8,1024]{2,1,0:T(8,128)S(1)}, u32[]{:S(2)}, u32[]{:S(2)}) %collective-permute-start.1) | collective-permute-done | bytes 65568 | tf_op jit(solution)/shard_map/ppermute | solution.py:116
  14.1 0.0 copy-done.2
  14.1 0.0 copy-start
  14.1 0.0 copy-start.1
  14.1 2.8 %collective-permute-start.5 = (f32[4,2,8,1024]{3,2,1,0:T(8,128)S(1)}, f32[4,2,8,1024]{3,2,1,0:T(8,128)S(1)}, u32[]{:S(2)}, u32[]{:S(2)}) collective-permute-start(f32[4,2,8,1024]{3,2,1,0:T(8,128)S(1)} %pad_maximum_fusion.refs_2_), channel_id=1, source_target_pairs={{0,48},{16,0},{32,16},{48,32},{64,112},{80,64},{96,80},{112,96},{1... | collective-permute-start | bytes 786440 | tf_op jit(solution)/shard_map/ppermute | solution.py:118
  16.9 0.3 collective-permute-start.4
  17.3 0.7 %collective-permute-start.3 = (f32[4,2,8,1024]{3,2,1,0:T(8,128)S(1)}, f32[4,2,8,1024]{3,2,1,0:T(8,128)S(1)}, u32[]{:S(2)}, u32[]{:S(2)}) collective-permute-start(f32[4,2,8,1024]{3,2,1,0:T(8,128)S(1)} %pad_maximum_fusion.refs_2_), channel_id=1, source_target_pairs={{0,16},{16,32},{32,48},{48,0},{64,80},{80,96},{96,112},{112,64},{1... | collective-permute-start | bytes 786440 | tf_op jit(solution)/shard_map/ppermute | solution.py:118
  18.0 0.0 copy-done
  18.0 0.0 copy-done.1
  18.0 0.5 prepare.1
  18.5 0.1 pad_add_fusion.refs_0_
  18.6 4.9 %collective-permute-done.5.refs_5_ = f32[4,2,8,1024]{3,2,1,0:T(8,128)S(1)} collective-permute-done((f32[4,2,8,1024]{3,2,1,0:T(8,128)S(1)}, f32[4,2,8,1024]{3,2,1,0:T(8,128)S(1)}, u32[]{:S(2)}, u32[]{:S(2)}) %collective-permute-start.5) | collective-permute-done | bytes 262176 | tf_op jit(solution)/shard_map/ppermute | solution.py:118
  23.4 0.4 collective-permute-done.4.refs_4_
  23.8 7.5 %collective-permute-done.3.refs_3_ = f32[4,2,8,1024]{3,2,1,0:T(8,128)S(1)} collective-permute-done((f32[4,2,8,1024]{3,2,1,0:T(8,128)S(1)}, f32[4,2,8,1024]{3,2,1,0:T(8,128)S(1)}, u32[]{:S(2)}, u32[]{:S(2)}) %collective-permute-start.3) | collective-permute-done | bytes 262176 | tf_op jit(solution)/shard_map/ppermute | solution.py:118
  31.3 4.5 %project.1 = f32[16,4,128]{2,1,0:T(4,128)S(1)} custom-call(s32[2]{0:T(128)S(1)} %pad_add_fusion.refs_0_, s32[8,16]{1,0:T(8,128)S(1)} %broadcast_shift-right-arithmetic_fusion.first_ref.refs_1_, f32[4,2,8,1024]{3,2,1,0:T(8,128)S(1)} %pad_maximum_fusion.refs_2_, f32[4,2,8,1024]{3,2,1,0:T(8,128)S(1)} %collective-permute-done.3.refs_3_, ...), custom_call_target="tpu_custom_call" | custom-call | tf_op jit(solution)/shard_map/project/pallas_call | solution.py:137
  35.8 14.3 %all_to_all.5 = f32[16,4,128]{2,1,0:T(4,128)S(1)} all-to-all(f32[16,4,128]{2,1,0:T(4,128)S(1)} %project.1), channel_id=1, replica_groups=mesh['tile'=16,'pulse'=16] {'pulse'}, dimensions={0} | all-to-all | bytes 65536 | tf_op jit(solution)/shard_map/all_to_all | solution.py:149
  50.1 0.6 %reshape.18 = f32[2,256]{1,0:T(2,128)} reshape(f32[4,128]{1,0:T(4,128)S(1)} %reduce_sum.19) | data formatting | bytes 4096 | tf_op jit(solution)/shard_map/reshape | solution.py:150
  (6 shorter events, 0.1 us)
Async XLA Ops:
  0.0 13.0 %collective-permute-start = (f32[2,8,1024]{2,1,0:T(8,128)}, f32[2,8,1024]{2,1,0:T(8,128)S(1)}, u32[]{:S(2)}, u32[]{:S(2)}) collective-permute-start(f32[2,8,1024]{2,1,0:T(8,128)} %param.3), channel_id=1, source_target_pairs={{0,64},{16,80},{32,96},{48,112},{64,128},{80,144},{96,160},{112,17... | collective-permute-start | bytes 196616 | tf_op jit(solution)/shard_map/ppermute | solution.py:116
  3.8 9.2 %collective-permute-start.2 = (f32[2,8,1024]{2,1,0:T(8,128)}, f32[2,8,1024]{2,1,0:T(8,128)S(1)}, u32[]{:S(2)}, u32[]{:S(2)}) collective-permute-start(f32[2,8,1024]{2,1,0:T(8,128)} %param.3), channel_id=1, source_target_pairs={{0,192},{16,208},{32,224},{48,240},{64,0},{80,16},{96,32},{112,48}... | collective-permute-start | bytes 196616 | tf_op jit(solution)/shard_map/ppermute | solution.py:116
  6.9 7.3 %collective-permute-start.1 = (f32[2,8,1024]{2,1,0:T(8,128)}, f32[2,8,1024]{2,1,0:T(8,128)S(1)}, u32[]{:S(2)}, u32[]{:S(2)}) collective-permute-start(f32[2,8,1024]{2,1,0:T(8,128)} %param.3), channel_id=1, source_target_pairs={{0,128},{16,144},{32,160},{48,176},{64,192},{80,208},{96,224},{112... | collective-permute-start | bytes 196616 | tf_op jit(solution)/shard_map/ppermute | solution.py:116
  11.6 2.5 %copy-start.2 = (f32[2,8,1024]{2,1,0:T(8,128)S(1)}, f32[2,8,1024]{2,1,0:T(8,128)}, u32[]{:S(2)}) copy-start(f32[2,8,1024]{2,1,0:T(8,128)} %param.3) | copy-start | bytes 196612
  14.1 3.9 %copy-start = (s32[8,4096]{1,0:T(8,128)S(1)}, s32[8,4096]{1,0:T(8,128)}, u32[]{:S(2)}) copy-start(s32[8,4096]{1,0:T(8,128)} %bins_ref.1) | copy-start | bytes 393220
  14.1 3.9 %copy-start.1 = (s32[8,4096]{1,0:T(8,128)S(1)}, s32[8,4096]{1,0:T(8,128)}, u32[]{:S(2)}) copy-start(s32[8,4096]{1,0:T(8,128)} %offsets_ref.1) | copy-start | bytes 393220
  14.1 9.3 %collective-permute-start.5 = (f32[4,2,8,1024]{3,2,1,0:T(8,128)S(1)}, f32[4,2,8,1024]{3,2,1,0:T(8,128)S(1)}, u32[]{:S(2)}, u32[]{:S(2)}) collective-permute-start(f32[4,2,8,1024]{3,2,1,0:T(8,128)S(1)} %pad_maximum_fusion.refs_2_), channel_id=1, source_target_pairs={{0,48},{16,0},{32,16},{48,32},{64,112},{80,64},{96,80},{112,96},{1... | collective-permute-start | bytes 786440 | tf_op jit(solution)/shard_map/ppermute | solution.py:118
  16.9 6.8 %collective-permute-start.4 = (f32[4,2,8,1024]{3,2,1,0:T(8,128)S(1)}, f32[4,2,8,1024]{3,2,1,0:T(8,128)S(1)}, u32[]{:S(2)}, u32[]{:S(2)}) collective-permute-start(f32[4,2,8,1024]{3,2,1,0:T(8,128)S(1)} %pad_maximum_fusion.refs_2_), channel_id=1, source_target_pairs={{0,32},{16,48},{32,0},{48,16},{64,96},{80,112},{96,64},{112,80},{1... | collective-permute-start | bytes 786440 | tf_op jit(solution)/shard_map/ppermute | solution.py:118
  17.3 14.0 %collective-permute-start.3 = (f32[4,2,8,1024]{3,2,1,0:T(8,128)S(1)}, f32[4,2,8,1024]{3,2,1,0:T(8,128)S(1)}, u32[]{:S(2)}, u32[]{:S(2)}) collective-permute-start(f32[4,2,8,1024]{3,2,1,0:T(8,128)S(1)} %pad_maximum_fusion.refs_2_), channel_id=1, source_target_pairs={{0,16},{16,32},{32,48},{48,0},{64,80},{80,96},{96,112},{112,64},{1... | collective-permute-start | bytes 786440 | tf_op jit(solution)/shard_map/ppermute | solution.py:118

commit v2 on v0

v2 whole, which is shorter than its diff:
```python
import math

import jax
import jax.numpy as jnp
from jax import lax
from jax.experimental import pallas as pl
from jax.experimental.pallas import tpu as pltpu
from jax.sharding import Mesh
from jax.sharding import PartitionSpec as P

TAPS = 8
FRAC = 16
BLOCK = 256
LANES = 128
SUBLANES = 8
SIDE = 4
AXES = ("far", "near", "x", "pair", "core")
SIZES = (4, 4, 4, 2, 2)


def tap_table():
    frac_part = jnp.arange(FRAC, dtype=jnp.float32)[:, None] / FRAC
    shift = jnp.arange(TAPS, dtype=jnp.float32)[None, :] - (TAPS // 2 - 1)
    offset = shift - frac_part
    values = jnp.sinc(offset) * (0.5 + 0.5 * jnp.cos(math.pi * offset / (TAPS // 2)))
    values = values / jnp.sum(values, axis=1, keepdims=True)
    return values.reshape(1, FRAC * TAPS)


def lane_take(row, index):
    return jnp.take_along_axis(row, index, axis=1, mode="promise_in_bounds")


def spread(row):
    return jnp.broadcast_to(row, (SUBLANES, LANES))


def cos_sin(steps):
    quarter = (steps + 512) >> 10
    x = (steps - (quarter << 10)).astype(jnp.float32) * (2.0 * math.pi / 4096.0)
    y = x * x
    s = x * (1.0 + y * (-1.0 / 6.0 + y * (1.0 / 120.0 + y * (-1.0 / 5040.0 + y * (1.0 / 362880.0)))))
    c = 1.0 + y * (-0.5 + y * (1.0 / 24.0 + y * (-1.0 / 720.0 + y * (1.0 / 40320.0))))
    odd = (quarter & 1) == 1
    cosine = jnp.where(odd, s, c)
    sine = jnp.where(odd, c, s)
    cosine = jnp.where(((quarter + 1) & 2) == 2, -cosine, cosine)
    sine = jnp.where((quarter & 2) == 2, -sine, sine)
    return cosine, sine


def arrange_kernel(near_ref, shard_ref, bins_ref, offsets_ref, *refs):
    *index_refs, out_ref, tiles = refs
    near = near_ref[0]
    lane = lax.broadcasted_iota(jnp.int32, (SUBLANES, LANES), 1)
    source = (lane & 15) * TAPS
    part = lane >> 4
    each = out_ref.shape[2]
    for c in range(2):
        rows = [shard_ref[c, :, t * LANES : (t + 1) * LANES] for t in range(TAPS)]
        for v in range(TAPS):
            got = lane_take(rows[0], source + v)
            for t in range(1, TAPS):
                got = jnp.where(part == t, lane_take(rows[t], source + v), got)
            tiles[c, :, v, :] = got
    quarters = SUBLANES // each
    length = index_refs[0].shape[2]
    for step, index_ref in enumerate(index_refs):
        for k, ref in enumerate((bins_ref, offsets_ref)):
            for p in range(each):
                pulse = pl.ds((near ^ step) * each + p, 1)
                for q in range(quarters):
                    row = p * quarters + q
                    index_ref[k, row : row + 1, :] = ref[pulse, q * length : (q + 1) * length]
    for c in range(2):
        for place in range(SIDE):
            for p in range(each):
                tile = tiles[c, place * each + p]
                for far in range(SIDE):
                    out_ref[far * SIDE + place, c, p] = tile


def prepare_kernel(scale, table_ref, index_ref, first_ref, real_ref, imag_ref, lane_ref):
    tiles, _, rows, length = index_ref.shape
    halves = BLOCK // LANES
    table = spread(table_ref[:, :])
    phase = lax.broadcasted_iota(jnp.int32, (SUBLANES, LANES), 0)
    for tile in range(tiles):
        for part in range(length // LANES):
            lanes = pl.ds(part * LANES, LANES)
            bins = index_ref[tile, 0, :, lanes]
            least = bins if part % halves == 0 else jnp.minimum(least, bins)
            if part % halves == halves - 1:
                block = part // halves
                lowest = jnp.min(least.astype(jnp.float32), axis=1, keepdims=True)
                first_ref[tile, :, block : block + 1] = lowest.astype(jnp.int32)
            fine = bins * FRAC + index_ref[tile, 1, :, lanes]
            cosine, sine = cos_sin((fine * 2861) & 4095)
            cosine, sine = cosine * scale, sine * scale
            for s in range(rows):
                fine_s = spread(fine[s : s + 1])
                bins_s = fine_s >> 4
                weight = lane_take(table, ((fine_s & 15) << 3) + ((phase - bins_s) & 7))
                real_ref[tile, s, part] = weight * spread(cosine[s : s + 1])
                imag_ref[tile, s, part] = weight * spread(sine[s : s + 1])
                lane_ref[tile, s, part] = ((bins_s - phase + 7) >> 3) & (LANES - 1)


def row_sums(values):
    row = lax.broadcasted_iota(jnp.int32, (SUBLANES, LANES), 0)
    low = (row & 4) == 0
    values = [jnp.where(low, a, b) + pltpu.roll(jnp.where(low, b, a), 4, 0) for a, b in zip(values[:4], values[4:])]
    for step in (2, 1):
        low = (row & step) == 0
        values = [
            jnp.where(low, a + pltpu.roll(a, SUBLANES - step, 0), b + pltpu.roll(b, step, 0))
            for a, b in zip(values[:step], values[step:])
        ]
    return values[0]


def project_kernel(near_ref, first_ref, whole, real_ref, imag_ref, lane_ref, out_ref):
    tiles, rows, parts = real_ref.shape[:3]
    owners, _, each = whole.shape[:3]
    quarters = rows // each
    halves = BLOCK // LANES
    column = lax.broadcasted_iota(jnp.int32, (SUBLANES, LANES), 1)
    for tile in range(tiles):
        for quarter in range(quarters):
            sums = []
            for block in range(parts // halves):
                total = [[jnp.zeros((SUBLANES, LANES), jnp.float32) for _ in range(halves)] for _ in range(2)]
                for p in range(each):
                    row = p * quarters + quarter
                    first = first_ref[tile, row, block]
                    owner = first >> 10
                    after = jnp.minimum(owner + 1, owners - 1)
                    here = column >= ((first >> 3) & (LANES - 1))
                    table = [jnp.where(here, whole[owner, c, p], whole[after, c, p]) for c in range(2)]
                    for half in range(halves):
                        part = block * halves + half
                        lane = lane_ref[tile, row, part]
                        got = [lane_take(table[c], lane) for c in range(2)]
                        real, imag = real_ref[tile, row, part], imag_ref[tile, row, part]
                        total[0][half] = total[0][half] + (got[0] * real - got[1] * imag)
                        total[1][half] = total[1][half] + (got[0] * imag + got[1] * real)
                sums += total[0] + total[1]
                if len(sums) == SUBLANES:
                    count = ((tile ^ near_ref[0]) * quarters + quarter) * (parts // halves) + block
                    out_ref[count // 2] = row_sums(sums)
                    sums = []


def swap(value, step):
    return lax.ppermute(value, "near", [(i, i ^ step) for i in range(SIDE)])


def local(profile, base_bin, tap_offset):
    pulses, pixels = base_bin.shape
    bins = profile.shape[2]
    each = pulses // SIDE
    quarters = SUBLANES // each
    length = pixels // quarters
    blocks, parts = length // BLOCK, length // LANES
    scale = 1.0 / math.sqrt(pulses * lax.axis_size(("x", "pair", "core")))
    vmem = pl.BlockSpec(memory_space=pltpu.VMEM)
    smem = pl.BlockSpec(memory_space=pltpu.SMEM)

    near = lax.axis_index("near").astype(jnp.int32).reshape(1)
    *index, shards = pl.pallas_call(
        arrange_kernel,
        out_shape=[jax.ShapeDtypeStruct((2, SUBLANES, length), jnp.int32)] * SIDE
        + [jax.ShapeDtypeStruct((SIDE * SIDE, 2, each, TAPS, bins // TAPS), jnp.float32)],
        in_specs=[smem] + [vmem] * 3,
        out_specs=[vmem] * (SIDE + 1),
        scratch_shapes=[pltpu.VMEM((2, pulses, TAPS, bins // TAPS), jnp.float32)],
        name="arrange",
    )(near, profile, base_bin, tap_offset)
    whole = lax.all_to_all(shards, ("far", "near"), 0, 0, tiled=True)
    index = jnp.stack([index[0]] + [swap(index[step], step) for step in range(1, SIDE)])
    by_part = (SIDE, SUBLANES, parts, TAPS, LANES)
    first, real, imag, lane = pl.pallas_call(
        lambda *refs: prepare_kernel(scale, *refs),
        out_shape=[
            jax.ShapeDtypeStruct((SIDE, SUBLANES, blocks), jnp.int32),
            jax.ShapeDtypeStruct(by_part, jnp.float32),
            jax.ShapeDtypeStruct(by_part, jnp.float32),
            jax.ShapeDtypeStruct(by_part, jnp.int32),
        ],
        in_specs=[vmem] * 2,
        out_specs=[vmem] * 4,
        cost_estimate=pl.CostEstimate(flops=pulses * pixels * 300, bytes_accessed=pulses * pixels * 104, transcendentals=0),
        compiler_params=pltpu.CompilerParams(vmem_limit_bytes=16 << 20),
        name="prepare",
    )(tap_table(), index)
    partial_image = pl.pallas_call(
        project_kernel,
        out_shape=jax.ShapeDtypeStruct((SIDE * pixels // BLOCK // 2, SUBLANES, LANES), jnp.float32),
        in_specs=[smem] * 2 + [vmem] * 4,
        out_specs=vmem,
        compiler_params=pltpu.CompilerParams(vmem_limit_bytes=24 << 20),
        name="project",
    )(near, first, whole, real, imag, lane)
    partial_image = partial_image.reshape(SIDE * pixels // BLOCK, 2 * BLOCK // LANES, LANES)
    received = lax.all_to_all(partial_image, ("near", "x", "pair", "core"), 0, 0, tiled=True)
    return jnp.sum(received, axis=0).reshape(2, BLOCK)


def solution(mesh):
    inner = Mesh(mesh.devices.reshape(SIZES), AXES)
    pulse, tile = ("x", "pair", "core"), ("far", "near")
    return jax.shard_map(
        local,
        mesh=inner,
        in_specs=(P(None, pulse, tile), P(pulse, tile), P(pulse, tile)),
        out_specs=P(None, tile + pulse),
        check_vma=False,
    )
```

time: 1230 us -> 45.2 us (0.04)
  waiting for transfers between devices: 763 us -> 5.04 us
  local copies, waits for them, and re-layouts: 330 us -> 0.86 us
  matrix products: 96.8 us -> 0 us
  blocking collectives: 0 us -> 17.6 us
  other arithmetic: 16.2 us -> 0.39 us
  starting transfers between devices: 0.04 us -> 15.8 us
  between operations: 14.9 us -> 0.07 us
    all_gather x1 -> x0, waiting for transfers between devices: 700 us -> none  [local(): whole = lax.all_gather(profile, 'tile', axis=2, tiled=True)]
    gather x16 -> x0, local copies, waits for them, and re-layouts: 273 us -> none  [backproject(): slabs = jnp.take(trace, indices, axis=1)]
    dot_general x16 -> x0, matrix products: 96.8 us -> none  [the longest x8 94.4 us: backproject(): jnp.einsum('cnw,nwb->cnb', slabs, banded, precision=lax.Precision.HIGHEST)]
    unnamed x3 -> x0, waiting for transfers between devices: 62.6 us -> none
    squeeze x1 -> x0, local copies, waits for them, and re-layouts: 44.5 us -> none  [backproject(): trace = whole[:, pulse_index, :]]
    all_to_all x0 -> x1, blocking collectives: none -> 17.6 us  [local(): lax.all_to_all(partial_image, ('near', 'x', 'pair', 'core'), 0, 0, tiled=...]
  transfers between devices with their start and end apart: 2 -> 4, of which waited for: 2 -> 2; matrix products, arithmetic and copies ran while one was open for 2% -> 1% of each run, Pallas kernels for 0% -> 2%
where the time goes in v2:
time: 45.2 us; the launch traced here: 45 us
  blocking collectives  17.6 us (39%)
  starting transfers between devices  15.8 us (35%)
  Pallas kernels  5.19 us (11%)
  waiting for transfers between devices  5.04 us (11%)
  local copies, waits for them, and re-layouts  0.86 us (2%)
    all_to_all x1, blocking collectives, local(): lax.all_to_all(partial_image, ('near', 'x', 'pair', 'core'), 0, 0, tiled=...  17.6 us
    all_to_all x1, starting transfers between devices, local(): whole = lax.all_to_all(shards, ('far', 'near'), 0, 0, tiled=True)  11.9 us
    ppermute x3, waiting for transfers between devices, swap(): return lax.ppermute(value, 'near', [(i, i ^ step) for i in range(SIDE)])  5.03 us
    ppermute x3, starting transfers between devices, swap(): return lax.ppermute(value, 'near', [(i, i ^ step) for i in range(SIDE)])  3.95 us
    pallas_call x1, Pallas kernels, local(): pl.pallas_call(project_kernel, out_shape=jax.ShapeDtypeStruct((SIDE * pix...  2.14 us
    pallas_call x1, Pallas kernels, local(): pl.pallas_call(arrange_kernel, out_shape=[jax.ShapeDtypeStruct((2, SUBLAN...  2.04 us
    pallas_call x1, Pallas kernels, local(): pl.pallas_call(lambda *refs: prepare_kernel(scale, *refs), out_shape=[jax...  1.01 us
  transfers between devices with their start and end apart: 4, of which 2 were waited for; matrix products, arithmetic and copies ran while one was open for 1% of the time, Pallas kernels for 2%

profile of v2, /device:TPU:1, one launch (start us, length us, event | category | flops | bytes accessed | tf_op | source)
XLA Modules:
  0.0 45.0 jit_solution(13121430219259060729)
XLA Ops:
  0.0 2.0 %arrange.1 = (s32[2,8,1024]{2,1,0:T(8,128)}, s32[2,8,1024]{2,1,0:T(8,128)}, s32[2,8,1024]{2,1,0:T(8,128)}, s32[2,8,1024]{2,1,0:T(8,128)}, f32[16,2,2,8,128]{4,3,2,1,0:T(8,128)}) custom-call(s32[1]{0:T(128)} %bitcast.near_ref, f32[2,8,1024]{2,1,0:T(8,128)} %shard_ref.1, s32[8,4096]{1,0:T(8,128)} %bins_ref.1, s32[8,4096]{1,0:T(8,128)} %offsets_ref.1), custom_call_target="tpu_custom_call" | custom-call | tf_op jit(solution)/shard_map/arrange/pallas_call | solution.py:170
  2.0 0.0 copy-start.3
  2.0 0.0 copy-start.2
  2.0 0.0 copy-start.1
  2.1 0.0 copy-start
  2.1 11.9 %all-to-all-start = ((f32[16,2,2,8,128]{4,3,2,1,0:T(8,128)}), f32[16,2,2,8,128]{4,3,2,1,0:T(8,128)S(1)}, u32[]{:S(2)}, u32[]{:S(2)}) async-start(f32[16,2,2,8,128]{4,3,2,1,0:T(8,128)} %get-tuple-element.19), calls=%async_computation | async-start | bytes 524288 | tf_op jit(solution)/shard_map/all_to_all | solution.py:179
  14.0 0.0 copy-done.3
  14.0 1.4 %collective-permute-start = (s32[2,8,1024]{2,1,0:T(8,128)S(1)}, s32[2,8,1024]{2,1,0:T(8,128)S(1)}, u32[]{:S(2)}, u32[]{:S(2)}) collective-permute-start(s32[2,8,1024]{2,1,0:T(8,128)S(1)} %copy-done.3), channel_id=1, source_target_pairs={{0,16},{16,0},{32,48},{48,32},{1,17},{17,1},{33,49},{49,33},{2,18}... | collective-permute-start | bytes 196616 | tf_op jit(solution)/shard_map/ppermute | solution.py:155
  15.4 0.0 copy-done.2
  15.4 2.4 %collective-permute-start.1 = (s32[2,8,1024]{2,1,0:T(8,128)S(1)}, s32[2,8,1024]{2,1,0:T(8,128)S(1)}, u32[]{:S(2)}, u32[]{:S(2)}) collective-permute-start(s32[2,8,1024]{2,1,0:T(8,128)S(1)} %copy-done.2), channel_id=1, source_target_pairs={{0,32},{16,48},{32,0},{48,16},{1,33},{17,49},{33,1},{49,17},{2,34}... | collective-permute-start | bytes 196616 | tf_op jit(solution)/shard_map/ppermute | solution.py:155
  17.8 0.0 copy-done.1
  17.8 0.1 collective-permute-start.2
  17.9 0.2 broadcast_subtract_fusion
  18.2 0.1 sub.64
  18.3 0.1 div.52
  18.3 0.1 div.53
  18.5 0.0 collective-permute-done
  18.5 2.6 %collective-permute-done.1 = s32[2,8,1024]{2,1,0:T(8,128)S(1)} collective-permute-done((s32[2,8,1024]{2,1,0:T(8,128)S(1)}, s32[2,8,1024]{2,1,0:T(8,128)S(1)}, u32[]{:S(2)}, u32[]{:S(2)}) %collective-permute-start.1) | collective-permute-done | bytes 65568 | tf_op jit(solution)/shard_map/ppermute | solution.py:155
  21.1 2.5 %collective-permute-done.2 = s32[2,8,1024]{2,1,0:T(8,128)S(1)} collective-permute-done((s32[2,8,1024]{2,1,0:T(8,128)S(1)}, s32[2,8,1024]{2,1,0:T(8,128)S(1)}, u32[]{:S(2)}, u32[]{:S(2)}) %collective-permute-start.2) | collective-permute-done | bytes 65568 | tf_op jit(solution)/shard_map/ppermute | solution.py:155
  23.5 0.0 copy-done
  23.6 1.0 %prepare.1 = (s32[4,8,4]{2,1,0:T(8,128)S(1)}, f32[4,8,8,8,128]{4,3,2,1,0:T(8,128)S(1)}, f32[4,8,8,8,128]{4,3,2,1,0:T(8,128)S(1)}, s32[4,8,8,8,128]{4,3,2,1,0:T(8,128)S(1)}) custom-call(f32[1,128]{1,0:T(1,128)S(1)} %fusion.30.refs_0_, s32[4,2,8,1024]{3,2,1,0:T(8,128)S(1)} %pad_add_fusion.refs_1_), custom_call_target="tpu_custom_call" | custom-call | flops 9830400 | bytes 3407872 | tf_op jit(solution)/shard_map/prepare/pallas_call | solution.py:182
  24.6 0.0 all-to-all-done.whole
  24.6 2.1 %project.1 = f32[32,8,128]{2,1,0:T(8,128)S(1)} custom-call(s32[1]{0:T(128)} %bitcast.near_ref, s32[4,8,4]{2,1,0:T(8,128)S(1)} %get-tuple-element.18.first_ref, f32[16,2,2,8,128]{4,3,2,1,0:T(8,128)S(1)} %all-to-all-done.whole, f32[4,8,8,8,128]{4,3,2,1,0:T(8,128)S(1)} %get-tuple-element.20.real_ref, f32[4,8,8,8,128]{4,3,2,1,0:T(8,128)S(1)} %get-tuple-element.21.imag_ref, ...), custom_call_target="tpu_custom_call" | custom-call | tf_op jit(solution)/shard_map/project/pallas_call | solution.py:196
  26.7 17.6 %all_to_all.10 = f32[64,4,128]{2,1,0:T(4,128)S(1)} all-to-all(f32[64,4,128]{2,1,0:T(4,128)S(1)} %bitcast.6), channel_id=1, replica_groups=mesh['far'=4,'near'=4,'x'=4,'pair'=2,'core'=2] {'near','x','pair','core'}, dimensions={0} | all-to-all | bytes 262144 | tf_op jit(solution)/shard_map/all_to_all | solution.py:205
  44.3 0.1 reduce_sum.19
  44.4 0.6 %reshape.171 = f32[2,256]{1,0:T(2,128)} reshape(f32[4,128]{1,0:T(4,128)S(1)} %reduce_sum.19) | data formatting | bytes 4096 | tf_op jit(solution)/shard_map/reshape | solution.py:206
  (4 shorter events, 0.1 us)
Async XLA Ops:
  2.0 11.9 %copy-start.3 = (s32[2,8,1024]{2,1,0:T(8,128)S(1)}, s32[2,8,1024]{2,1,0:T(8,128)}, u32[]{:S(2)}) copy-start(s32[2,8,1024]{2,1,0:T(8,128)} %get-tuple-element.15) | copy-start | bytes 196612
  2.0 13.4 %copy-start.2 = (s32[2,8,1024]{2,1,0:T(8,128)S(1)}, s32[2,8,1024]{2,1,0:T(8,128)}, u32[]{:S(2)}) copy-start(s32[2,8,1024]{2,1,0:T(8,128)} %get-tuple-element.16) | copy-start | bytes 196612
  2.0 15.8 %copy-start.1 = (s32[2,8,1024]{2,1,0:T(8,128)S(1)}, s32[2,8,1024]{2,1,0:T(8,128)}, u32[]{:S(2)}) copy-start(s32[2,8,1024]{2,1,0:T(8,128)} %get-tuple-element.17) | copy-start | bytes 196612
  2.1 21.5 %copy-start = (s32[2,8,1024]{2,1,0:T(8,128)S(1)}, s32[2,8,1024]{2,1,0:T(8,128)}, u32[]{:S(2)}) copy-start(s32[2,8,1024]{2,1,0:T(8,128)} %get-tuple-element.14) | copy-start | bytes 196612
  2.1 22.5 %all-to-all-start = ((f32[16,2,2,8,128]{4,3,2,1,0:T(8,128)}), f32[16,2,2,8,128]{4,3,2,1,0:T(8,128)S(1)}, u32[]{:S(2)}, u32[]{:S(2)}) async-start(f32[16,2,2,8,128]{4,3,2,1,0:T(8,128)} %get-tuple-element.19), calls=%async_computation | async-start | bytes 524288 | tf_op jit(solution)/shard_map/all_to_all | solution.py:179
  14.0 4.5 %collective-permute-start = (s32[2,8,1024]{2,1,0:T(8,128)S(1)}, s32[2,8,1024]{2,1,0:T(8,128)S(1)}, u32[]{:S(2)}, u32[]{:S(2)}) collective-permute-start(s32[2,8,1024]{2,1,0:T(8,128)S(1)} %copy-done.3), channel_id=1, source_target_pairs={{0,16},{16,0},{32,48},{48,32},{1,17},{17,1},{33,49},{49,33},{2,18}... | collective-permute-start | bytes 196616 | tf_op jit(solution)/shard_map/ppermute | solution.py:155
  15.4 5.6 %collective-permute-start.1 = (s32[2,8,1024]{2,1,0:T(8,128)S(1)}, s32[2,8,1024]{2,1,0:T(8,128)S(1)}, u32[]{:S(2)}, u32[]{:S(2)}) collective-permute-start(s32[2,8,1024]{2,1,0:T(8,128)S(1)} %copy-done.2), channel_id=1, source_target_pairs={{0,32},{16,48},{32,0},{48,16},{1,33},{17,49},{33,1},{49,17},{2,34}... | collective-permute-start | bytes 196616 | tf_op jit(solution)/shard_map/ppermute | solution.py:155
  17.8 5.7 %collective-permute-start.2 = (s32[2,8,1024]{2,1,0:T(8,128)S(1)}, s32[2,8,1024]{2,1,0:T(8,128)S(1)}, u32[]{:S(2)}, u32[]{:S(2)}) collective-permute-start(s32[2,8,1024]{2,1,0:T(8,128)S(1)} %copy-done.1), channel_id=1, source_target_pairs={{0,48},{16,32},{32,16},{48,0},{1,49},{17,33},{33,17},{49,1},{2,50}... | collective-permute-start | bytes 196616 | tf_op jit(solution)/shard_map/ppermute | solution.py:155

commit v3 on v2

--- a/solution.py
+++ b/solution.py
@@ -49,9 +49,9 @@
     return cosine, sine
 
 
-def arrange_kernel(near_ref, shard_ref, bins_ref, offsets_ref, *refs):
+def arrange_kernel(shard_ref, bins_ref, offsets_ref, *refs):
     *index_refs, out_ref, tiles = refs
-    near = near_ref[0]
+    near = lax.axis_index("near")
     lane = lax.broadcasted_iota(jnp.int32, (SUBLANES, LANES), 1)
     source = (lane & 15) * TAPS
     part = lane >> 4
@@ -93,7 +93,8 @@
             if part % halves == halves - 1:
                 block = part // halves
                 lowest = jnp.min(least.astype(jnp.float32), axis=1, keepdims=True)
-                first_ref[tile, :, block : block + 1] = lowest.astype(jnp.int32)
+                count = tile * (length // BLOCK) + block
+                first_ref[:, count : count + 1] = lowest.astype(jnp.int32)
             fine = bins * FRAC + index_ref[tile, 1, :, lanes]
             cosine, sine = cos_sin((fine * 2861) & 4095)
             cosine, sine = cosine * scale, sine * scale
@@ -119,20 +120,23 @@
     return values[0]
 
 
-def project_kernel(near_ref, first_ref, whole, real_ref, imag_ref, lane_ref, out_ref):
+def project_kernel(own, first_ref, whole, real_ref, imag_ref, lane_ref, out_ref):
     tiles, rows, parts = real_ref.shape[:3]
     owners, _, each = whole.shape[:3]
     quarters = rows // each
     halves = BLOCK // LANES
+    near, core = lax.axis_index("near"), lax.axis_index("core")
+    parity = core if own else 1 - core
     column = lax.broadcasted_iota(jnp.int32, (SUBLANES, LANES), 1)
     for tile in range(tiles):
         for quarter in range(quarters):
             sums = []
-            for block in range(parts // halves):
+            for pair in range(parts // halves // 2):
+                block = 2 * pair + parity
                 total = [[jnp.zeros((SUBLANES, LANES), jnp.float32) for _ in range(halves)] for _ in range(2)]
                 for p in range(each):
                     row = p * quarters + quarter
-                    first = first_ref[tile, row, block]
+                    first = first_ref[row, tile * (parts // halves) + block]
                     owner = first >> 10
                     after = jnp.minimum(owner + 1, owners - 1)
                     here = column >= ((first >> 3) & (LANES - 1))
@@ -145,10 +149,7 @@
                         total[0][half] = total[0][half] + (got[0] * real - got[1] * imag)
                         total[1][half] = total[1][half] + (got[0] * imag + got[1] * real)
                 sums += total[0] + total[1]
-                if len(sums) == SUBLANES:
-                    count = ((tile ^ near_ref[0]) * quarters + quarter) * (parts // halves) + block
-                    out_ref[count // 2] = row_sums(sums)
-                    sums = []
+            out_ref[(tile ^ near) * quarters + quarter] = row_sums(sums)
 
 
 def swap(value, step):
@@ -166,23 +167,22 @@
     vmem = pl.BlockSpec(memory_space=pltpu.VMEM)
     smem = pl.BlockSpec(memory_space=pltpu.SMEM)
 
-    near = lax.axis_index("near").astype(jnp.int32).reshape(1)
     *index, shards = pl.pallas_call(
         arrange_kernel,
         out_shape=[jax.ShapeDtypeStruct((2, SUBLANES, length), jnp.int32)] * SIDE
         + [jax.ShapeDtypeStruct((SIDE * SIDE, 2, each, TAPS, bins // TAPS), jnp.float32)],
-        in_specs=[smem] + [vmem] * 3,
+        in_specs=[vmem] * 3,
         out_specs=[vmem] * (SIDE + 1),
         scratch_shapes=[pltpu.VMEM((2, pulses, TAPS, bins // TAPS), jnp.float32)],
         name="arrange",
-    )(near, profile, base_bin, tap_offset)
+    )(profile, base_bin, tap_offset)
     whole = lax.all_to_all(shards, ("far", "near"), 0, 0, tiled=True)
     index = jnp.stack([index[0]] + [swap(index[step], step) for step in range(1, SIDE)])
     by_part = (SIDE, SUBLANES, parts, TAPS, LANES)
     first, real, imag, lane = pl.pallas_call(
         lambda *refs: prepare_kernel(scale, *refs),
         out_shape=[
-            jax.ShapeDtypeStruct((SIDE, SUBLANES, blocks), jnp.int32),
+            jax.ShapeDtypeStruct((SUBLANES, SIDE * blocks), jnp.int32),
             jax.ShapeDtypeStruct(by_part, jnp.float32),
             jax.ShapeDtypeStruct(by_part, jnp.float32),
             jax.ShapeDtypeStruct(by_part, jnp.int32),
@@ -193,16 +193,20 @@
         compiler_params=pltpu.CompilerParams(vmem_limit_bytes=16 << 20),
         name="prepare",
     )(tap_table(), index)
-    partial_image = pl.pallas_call(
-        project_kernel,
-        out_shape=jax.ShapeDtypeStruct((SIDE * pixels // BLOCK // 2, SUBLANES, LANES), jnp.float32),
-        in_specs=[smem] * 2 + [vmem] * 4,
-        out_specs=vmem,
-        compiler_params=pltpu.CompilerParams(vmem_limit_bytes=24 << 20),
-        name="project",
-    )(near, first, whole, real, imag, lane)
-    partial_image = partial_image.reshape(SIDE * pixels // BLOCK, 2 * BLOCK // LANES, LANES)
-    received = lax.all_to_all(partial_image, ("near", "x", "pair", "core"), 0, 0, tiled=True)
+    def project(own):
+        return pl.pallas_call(
+            lambda *refs: project_kernel(own, *refs),
+            out_shape=jax.ShapeDtypeStruct((SIDE * quarters, SUBLANES, LANES), jnp.float32),
+            in_specs=[smem] + [vmem] * 4,
+            out_specs=vmem,
+            cost_estimate=pl.CostEstimate(flops=1 << 24, bytes_accessed=2 << 20, transcendentals=0),
+            compiler_params=pltpu.CompilerParams(vmem_limit_bytes=24 << 20),
+            name="project",
+        )(first, whole, real, imag, lane)
+
+    theirs = lax.ppermute(project(False), "core", [(0, 1), (1, 0)])
+    partial_image = (project(True) + theirs).reshape(SIDE * pixels // BLOCK // 2, 2 * BLOCK // LANES, LANES)
+    received = lax.all_to_all(partial_image, ("near", "x", "pair"), 0, 0, tiled=True)
     return jnp.sum(received, axis=0).reshape(2, BLOCK)
 
 

time: 45.2 us -> 44.2 us (0.978)
  blocking collectives: 17.6 us -> 13 us
  starting transfers between devices: 15.8 us -> 18.9 us
  Pallas kernels: 5.19 us -> 5.68 us
    all_to_all x1, blocking collectives: 17.6 us -> 13 us  [local(): lax.all_to_all(partial_image, ('near', 'x', 'pair'), 0, 0, tiled=True)]
    ppermute x0 -> x1, starting transfers between devices: none -> 3.06 us  [local(): theirs = lax.ppermute(project(False), 'core', [(0, 1), (1, 0)])]
    pallas_call x1 -> x2, Pallas kernels: 2.14 us -> 2.63 us  [project(): pl.pallas_call(lambda *refs: project_kernel(own, *refs), out_shape=jax.Sh...]
  transfers between devices with their start and end apart: 4 -> 5, of which waited for: 2 -> 2; matrix products, arithmetic and copies ran while one was open for 1% -> 1% of each run, Pallas kernels for 2% -> 5%
where the time goes in v3:
time: 44.2 us; the launch traced here: 43.9 us
  starting transfers between devices  18.9 us (43%)
  blocking collectives  13 us (29%)
  Pallas kernels  5.68 us (13%)
  waiting for transfers between devices  5.04 us (11%)
  local copies, waits for them, and re-layouts  0.86 us (2%)
    all_to_all x1, blocking collectives, local(): lax.all_to_all(partial_image, ('near', 'x', 'pair'), 0, 0, tiled=True)  13 us
    all_to_all x1, starting transfers between devices, local(): whole = lax.all_to_all(shards, ('far', 'near'), 0, 0, tiled=True)  11.9 us
    ppermute x3, waiting for transfers between devices, swap(): return lax.ppermute(value, 'near', [(i, i ^ step) for i in range(SIDE)])  5.03 us
    ppermute x3, starting transfers between devices, swap(): return lax.ppermute(value, 'near', [(i, i ^ step) for i in range(SIDE)])  3.95 us
    ppermute x1, starting transfers between devices, local(): theirs = lax.ppermute(project(False), 'core', [(0, 1), (1, 0)])  3.06 us
    pallas_call x2, Pallas kernels, project(): pl.pallas_call(lambda *refs: project_kernel(own, *refs), out_shape=jax.Sh...  2.63 us
    pallas_call x1, Pallas kernels, local(): pl.pallas_call(arrange_kernel, out_shape=[jax.ShapeDtypeStruct((2, SUBLAN...  2.03 us
    pallas_call x1, Pallas kernels, local(): pl.pallas_call(lambda *refs: prepare_kernel(scale, *refs), out_shape=[jax...  1.01 us
  transfers between devices with their start and end apart: 5, of which 2 were waited for; matrix products, arithmetic and copies ran while one was open for 1% of the time, Pallas kernels for 5%

profile of v3, /device:TPU:1, one launch (start us, length us, event | category | flops | bytes accessed | tf_op | source)
XLA Modules:
  0.0 43.9 jit_solution(17678592415685019470)
XLA Ops:
  0.0 2.0 %arrange.1 = (s32[2,8,1024]{2,1,0:T(8,128)}, s32[2,8,1024]{2,1,0:T(8,128)}, s32[2,8,1024]{2,1,0:T(8,128)}, s32[2,8,1024]{2,1,0:T(8,128)}, f32[16,2,2,8,128]{4,3,2,1,0:T(8,128)}) custom-call(f32[2,8,1024]{2,1,0:T(8,128)} %shard_ref.1, s32[8,4096]{1,0:T(8,128)} %bins_ref.1, s32[8,4096]{1,0:T(8,128)} %offsets_ref.1), custom_call_target="tpu_custom_call" | custom-call | tf_op jit(solution)/shard_map/arrange/pallas_call | solution.py:170
  2.0 0.0 copy-start.3
  2.0 0.0 copy-start.2
  2.0 0.0 copy-start.1
  2.0 0.0 copy-start
  2.1 11.9 %all-to-all-start = ((f32[16,2,2,8,128]{4,3,2,1,0:T(8,128)}), f32[16,2,2,8,128]{4,3,2,1,0:T(8,128)S(1)}, u32[]{:S(2)}, u32[]{:S(2)}) async-start(f32[16,2,2,8,128]{4,3,2,1,0:T(8,128)} %get-tuple-element.19), calls=%async_computation | async-start | bytes 524288 | tf_op jit(solution)/shard_map/all_to_all | solution.py:179
  14.0 0.0 copy-done.3
  14.0 1.4 %collective-permute-start = (s32[2,8,1024]{2,1,0:T(8,128)S(1)}, s32[2,8,1024]{2,1,0:T(8,128)S(1)}, u32[]{:S(2)}, u32[]{:S(2)}) collective-permute-start(s32[2,8,1024]{2,1,0:T(8,128)S(1)} %copy-done.3), channel_id=1, source_target_pairs={{0,16},{16,0},{32,48},{48,32},{1,17},{17,1},{33,49},{49,33},{2,18}... | collective-permute-start | bytes 196616 | tf_op jit(solution)/shard_map/ppermute | solution.py:156
  15.4 0.0 copy-done.2
  15.4 2.4 %collective-permute-start.1 = (s32[2,8,1024]{2,1,0:T(8,128)S(1)}, s32[2,8,1024]{2,1,0:T(8,128)S(1)}, u32[]{:S(2)}, u32[]{:S(2)}) collective-permute-start(s32[2,8,1024]{2,1,0:T(8,128)S(1)} %copy-done.2), channel_id=1, source_target_pairs={{0,32},{16,48},{32,0},{48,16},{1,33},{17,49},{33,1},{49,17},{2,34}... | collective-permute-start | bytes 196616 | tf_op jit(solution)/shard_map/ppermute | solution.py:156
  17.8 0.0 copy-done.1
  17.8 0.1 collective-permute-start.2
  17.9 0.2 broadcast_subtract_fusion
  18.2 0.1 sub.64
  18.3 0.1 div.52
  18.3 0.1 div.53
  18.5 0.0 collective-permute-done
  18.5 2.6 %collective-permute-done.1 = s32[2,8,1024]{2,1,0:T(8,128)S(1)} collective-permute-done((s32[2,8,1024]{2,1,0:T(8,128)S(1)}, s32[2,8,1024]{2,1,0:T(8,128)S(1)}, u32[]{:S(2)}, u32[]{:S(2)}) %collective-permute-start.1) | collective-permute-done | bytes 65568 | tf_op jit(solution)/shard_map/ppermute | solution.py:156
  21.0 2.5 %collective-permute-done.2 = s32[2,8,1024]{2,1,0:T(8,128)S(1)} collective-permute-done((s32[2,8,1024]{2,1,0:T(8,128)S(1)}, s32[2,8,1024]{2,1,0:T(8,128)S(1)}, u32[]{:S(2)}, u32[]{:S(2)}) %collective-permute-start.2) | collective-permute-done | bytes 65568 | tf_op jit(solution)/shard_map/ppermute | solution.py:156
  23.5 0.0 copy-done
  23.5 1.0 %prepare.1 = (s32[8,16]{1,0:T(8,128)S(1)}, f32[4,8,8,8,128]{4,3,2,1,0:T(8,128)S(1)}, f32[4,8,8,8,128]{4,3,2,1,0:T(8,128)S(1)}, s32[4,8,8,8,128]{4,3,2,1,0:T(8,128)S(1)}) custom-call(f32[1,128]{1,0:T(1,128)S(1)} %fusion.30.refs_0_, s32[4,2,8,1024]{3,2,1,0:T(8,128)S(1)} %pad_add_fusion.refs_1_), custom_call_target="tpu_custom_call" | custom-call | flops 9830400 | bytes 3407872 | tf_op jit(solution)/shard_map/prepare/pallas_call | solution.py:182
  24.6 0.0 all-to-all-done.refs_1_
  24.6 1.3 %project.3 = f32[16,8,128]{2,1,0:T(8,128)S(1)} custom-call(s32[8,16]{1,0:T(8,128)S(1)} %get-tuple-element.18.refs_0_, f32[16,2,2,8,128]{4,3,2,1,0:T(8,128)S(1)} %all-to-all-done.refs_1_, f32[4,8,8,8,128]{4,3,2,1,0:T(8,128)S(1)} %get-tuple-element.20.refs_2_, f32[4,8,8,8,128]{4,3,2,1,0:T(8,128)S(1)} %get-tuple-element.21.refs_3_, ...), custom_call_target="tpu_custom_call" | custom-call | flops 16777216 | bytes 2097152 | tf_op jit(solution)/shard_map/project/pallas_call | solution.py:197
  25.9 3.1 %collective-permute-start.3 = (f32[16,8,128]{2,1,0:T(8,128)S(1)}, f32[16,8,128]{2,1,0:T(8,128)S(1)}, u32[]{:S(2)}, u32[]{:S(2)}) collective-permute-start(f32[16,8,128]{2,1,0:T(8,128)S(1)} %project.3), channel_id=1, source_target_pairs={{0,1},{1,0},{2,3},{3,2},{4,5},{5,4},{6,7},{7,6},{8,9},{9,8},{10,11... | collective-permute-start | bytes 196616 | tf_op jit(solution)/shard_map/ppermute | solution.py:207
  28.9 1.3 %project.2 = f32[16,8,128]{2,1,0:T(8,128)S(1)} custom-call(s32[8,16]{1,0:T(8,128)S(1)} %get-tuple-element.18.refs_0_, f32[16,2,2,8,128]{4,3,2,1,0:T(8,128)S(1)} %all-to-all-done.refs_1_, f32[4,8,8,8,128]{4,3,2,1,0:T(8,128)S(1)} %get-tuple-element.20.refs_2_, f32[4,8,8,8,128]{4,3,2,1,0:T(8,128)S(1)} %get-tuple-element.21.refs_3_, ...), custom_call_target="tpu_custom_call" | custom-call | flops 16777216 | bytes 2097152 | tf_op jit(solution)/shard_map/project/pallas_call | solution.py:197
  30.3 0.0 collective-permute-done.3
  30.3 13.0 %all_to_all.10 = f32[32,4,128]{2,1,0:T(4,128)S(1)} all-to-all(f32[32,4,128]{2,1,0:T(4,128)S(1)} %bitcast.5), channel_id=1, replica_groups=mesh['far'=4,'near'=4,'x'=4,'pair'=2,'core'=2] {'near','x','pair'}, dimensions={0} | all-to-all | bytes 131072 | tf_op jit(solution)/shard_map/all_to_all | solution.py:209
  43.3 0.6 %reshape.167 = f32[2,256]{1,0:T(2,128)} reshape(f32[4,128]{1,0:T(4,128)S(1)} %reduce_sum.19) | data formatting | bytes 4096 | tf_op jit(solution)/shard_map/reshape | solution.py:210
  (6 shorter events, 0.1 us)
Async XLA Ops:
  2.0 11.9 %copy-start.3 = (s32[2,8,1024]{2,1,0:T(8,128)S(1)}, s32[2,8,1024]{2,1,0:T(8,128)}, u32[]{:S(2)}) copy-start(s32[2,8,1024]{2,1,0:T(8,128)} %get-tuple-element.15) | copy-start | bytes 196612
  2.0 13.4 %copy-start.2 = (s32[2,8,1024]{2,1,0:T(8,128)S(1)}, s32[2,8,1024]{2,1,0:T(8,128)}, u32[]{:S(2)}) copy-start(s32[2,8,1024]{2,1,0:T(8,128)} %get-tuple-element.16) | copy-start | bytes 196612
  2.0 15.8 %copy-start.1 = (s32[2,8,1024]{2,1,0:T(8,128)S(1)}, s32[2,8,1024]{2,1,0:T(8,128)}, u32[]{:S(2)}) copy-start(s32[2,8,1024]{2,1,0:T(8,128)} %get-tuple-element.17) | copy-start | bytes 196612
  2.0 21.5 %copy-start = (s32[2,8,1024]{2,1,0:T(8,128)S(1)}, s32[2,8,1024]{2,1,0:T(8,128)}, u32[]{:S(2)}) copy-start(s32[2,8,1024]{2,1,0:T(8,128)} %get-tuple-element.14) | copy-start | bytes 196612
  2.1 22.5 %all-to-all-start = ((f32[16,2,2,8,128]{4,3,2,1,0:T(8,128)}), f32[16,2,2,8,128]{4,3,2,1,0:T(8,128)S(1)}, u32[]{:S(2)}, u32[]{:S(2)}) async-start(f32[16,2,2,8,128]{4,3,2,1,0:T(8,128)} %get-tuple-element.19), calls=%async_computation | async-start | bytes 524288 | tf_op jit(solution)/shard_map/all_to_all | solution.py:179
  14.0 4.5 %collective-permute-start = (s32[2,8,1024]{2,1,0:T(8,128)S(1)}, s32[2,8,1024]{2,1,0:T(8,128)S(1)}, u32[]{:S(2)}, u32[]{:S(2)}) collective-permute-start(s32[2,8,1024]{2,1,0:T(8,128)S(1)} %copy-done.3), channel_id=1, source_target_pairs={{0,16},{16,0},{32,48},{48,32},{1,17},{17,1},{33,49},{49,33},{2,18}... | collective-permute-start | bytes 196616 | tf_op jit(solution)/shard_map/ppermute | solution.py:156
  15.4 5.6 %collective-permute-start.1 = (s32[2,8,1024]{2,1,0:T(8,128)S(1)}, s32[2,8,1024]{2,1,0:T(8,128)S(1)}, u32[]{:S(2)}, u32[]{:S(2)}) collective-permute-start(s32[2,8,1024]{2,1,0:T(8,128)S(1)} %copy-done.2), channel_id=1, source_target_pairs={{0,32},{16,48},{32,0},{48,16},{1,33},{17,49},{33,1},{49,17},{2,34}... | collective-permute-start | bytes 196616 | tf_op jit(solution)/shard_map/ppermute | solution.py:156
  17.8 5.7 %collective-permute-start.2 = (s32[2,8,1024]{2,1,0:T(8,128)S(1)}, s32[2,8,1024]{2,1,0:T(8,128)S(1)}, u32[]{:S(2)}, u32[]{:S(2)}) collective-permute-start(s32[2,8,1024]{2,1,0:T(8,128)S(1)} %copy-done.1), channel_id=1, source_target_pairs={{0,48},{16,32},{32,16},{48,0},{1,49},{17,33},{33,17},{49,1},{2,50}... | collective-permute-start | bytes 196616 | tf_op jit(solution)/shard_map/ppermute | solution.py:156
  25.9 4.4 %collective-permute-start.3 = (f32[16,8,128]{2,1,0:T(8,128)S(1)}, f32[16,8,128]{2,1,0:T(8,128)S(1)}, u32[]{:S(2)}, u32[]{:S(2)}) collective-permute-start(f32[16,8,128]{2,1,0:T(8,128)S(1)} %project.3), channel_id=1, source_target_pairs={{0,1},{1,0},{2,3},{3,2},{4,5},{5,4},{6,7},{7,6},{8,9},{9,8},{10,11... | collective-permute-start | bytes 196616 | tf_op jit(solution)/shard_map/ppermute | solution.py:207

commit v4 on v3

--- a/solution.py
+++ b/solution.py
@@ -80,22 +80,24 @@
                     out_ref[far * SIDE + place, c, p] = tile
 
 
-def prepare_kernel(scale, table_ref, index_ref, first_ref, real_ref, imag_ref, lane_ref):
+def prepare_kernel(scale, table_ref, index_ref, first_ref, real_ref, imag_ref, lane_ref, lowest_ref, sem):
     tiles, _, rows, length = index_ref.shape
     halves = BLOCK // LANES
     table = spread(table_ref[:, :])
     phase = lax.broadcasted_iota(jnp.int32, (SUBLANES, LANES), 0)
+    lowest_ref[:, :] = jnp.zeros(lowest_ref.shape, jnp.int32)
+    for tile in range(tiles):
+        for block in range(length // BLOCK):
+            pair = [index_ref[tile, 0, :, (block * halves + h) * LANES : (block * halves + h + 1) * LANES] for h in range(halves)]
+            lowest = jnp.min(jnp.minimum(*pair).astype(jnp.float32), axis=1, keepdims=True)
+            count = tile * (length // BLOCK) + block
+            lowest_ref[:, count : count + 1] = lowest.astype(jnp.int32)
+    copy = pltpu.make_async_copy(lowest_ref, first_ref, sem)
+    copy.start()
     for tile in range(tiles):
         for part in range(length // LANES):
             lanes = pl.ds(part * LANES, LANES)
-            bins = index_ref[tile, 0, :, lanes]
-            least = bins if part % halves == 0 else jnp.minimum(least, bins)
-            if part % halves == halves - 1:
-                block = part // halves
-                lowest = jnp.min(least.astype(jnp.float32), axis=1, keepdims=True)
-                count = tile * (length // BLOCK) + block
-                first_ref[:, count : count + 1] = lowest.astype(jnp.int32)
-            fine = bins * FRAC + index_ref[tile, 1, :, lanes]
+            fine = index_ref[tile, 0, :, lanes] * FRAC + index_ref[tile, 1, :, lanes]
             cosine, sine = cos_sin((fine * 2861) & 4095)
             cosine, sine = cosine * scale, sine * scale
             for s in range(rows):
@@ -105,6 +107,7 @@
                 real_ref[tile, s, part] = weight * spread(cosine[s : s + 1])
                 imag_ref[tile, s, part] = weight * spread(sine[s : s + 1])
                 lane_ref[tile, s, part] = ((bins_s - phase + 7) >> 3) & (LANES - 1)
+    copy.wait()
 
 
 def row_sums(values):
@@ -182,13 +185,14 @@
     first, real, imag, lane = pl.pallas_call(
         lambda *refs: prepare_kernel(scale, *refs),
         out_shape=[
-            jax.ShapeDtypeStruct((SUBLANES, SIDE * blocks), jnp.int32),
+            pltpu.SMEM((SUBLANES, LANES), jnp.int32),
             jax.ShapeDtypeStruct(by_part, jnp.float32),
             jax.ShapeDtypeStruct(by_part, jnp.float32),
             jax.ShapeDtypeStruct(by_part, jnp.int32),
         ],
         in_specs=[vmem] * 2,
-        out_specs=[vmem] * 4,
+        out_specs=[smem] + [vmem] * 3,
+        scratch_shapes=[pltpu.VMEM((SUBLANES, LANES), jnp.int32), pltpu.SemaphoreType.DMA],
         cost_estimate=pl.CostEstimate(flops=pulses * pixels * 300, bytes_accessed=pulses * pixels * 104, transcendentals=0),
         compiler_params=pltpu.CompilerParams(vmem_limit_bytes=16 << 20),
         name="prepare",

time: 44.2 us -> 43.1 us (0.975)
  Pallas kernels: 5.68 us -> 4.94 us
  starting transfers between devices: 18.9 us -> 18.4 us
    pallas_call x2, Pallas kernels: 2.63 us -> 1.43 us  [project(): pl.pallas_call(lambda *refs: project_kernel(own, *refs), out_shape=jax.Sh...]
    ppermute x1, starting transfers between devices: 3.06 us -> 2.58 us  [local(): theirs = lax.ppermute(project(False), 'core', [(0, 1), (1, 0)])]
    pallas_call x1, Pallas kernels: 1.01 us -> 1.47 us  [local(): pl.pallas_call(lambda *refs: prepare_kernel(scale, *refs), out_shape=[plt...]
  transfers between devices with their start and end apart: 5 -> 5, of which waited for: 2 -> 3; matrix products, arithmetic and copies ran while one was open for 1% -> 1% of each run, Pallas kernels for 5% -> 5%
where the time goes in v4:
time: 43.1 us; the launch traced here: 42.8 us
  starting transfers between devices  18.4 us (43%)
  blocking collectives  12.9 us (30%)
  waiting for transfers between devices  5.22 us (12%)
  Pallas kernels  4.94 us (11%)
  local copies, waits for them, and re-layouts  0.86 us (2%)
    all_to_all x1, blocking collectives, local(): lax.all_to_all(partial_image, ('near', 'x', 'pair'), 0, 0, tiled=True)  12.9 us
    all_to_all x1, starting transfers between devices, local(): whole = lax.all_to_all(shards, ('far', 'near'), 0, 0, tiled=True)  11.9 us
    ppermute x3, waiting for transfers between devices, swap(): return lax.ppermute(value, 'near', [(i, i ^ step) for i in range(SIDE)])  5.03 us
    ppermute x3, starting transfers between devices, swap(): return lax.ppermute(value, 'near', [(i, i ^ step) for i in range(SIDE)])  3.95 us
    ppermute x1, starting transfers between devices, local(): theirs = lax.ppermute(project(False), 'core', [(0, 1), (1, 0)])  2.58 us
    pallas_call x1, Pallas kernels, local(): pl.pallas_call(arrange_kernel, out_shape=[jax.ShapeDtypeStruct((2, SUBLAN...  2.03 us
    pallas_call x1, Pallas kernels, local(): pl.pallas_call(lambda *refs: prepare_kernel(scale, *refs), out_shape=[plt...  1.47 us
    pallas_call x2, Pallas kernels, project(): pl.pallas_call(lambda *refs: project_kernel(own, *refs), out_shape=jax.Sh...  1.43 us
  transfers between devices with their start and end apart: 5, of which 3 were waited for; matrix products, arithmetic and copies ran while one was open for 1% of the time, Pallas kernels for 5%

profile of v4, /device:TPU:1, one launch (start us, length us, event | category | flops | bytes accessed | tf_op | source)
XLA Modules:
  0.0 42.8 jit_solution(5877186619016507100)
XLA Ops:
  0.0 2.0 %arrange.1 = (s32[2,8,1024]{2,1,0:T(8,128)}, s32[2,8,1024]{2,1,0:T(8,128)}, s32[2,8,1024]{2,1,0:T(8,128)}, s32[2,8,1024]{2,1,0:T(8,128)}, f32[16,2,2,8,128]{4,3,2,1,0:T(8,128)}) custom-call(f32[2,8,1024]{2,1,0:T(8,128)} %shard_ref.1, s32[8,4096]{1,0:T(8,128)} %bins_ref.1, s32[8,4096]{1,0:T(8,128)} %offsets_ref.1), custom_call_target="tpu_custom_call" | custom-call | tf_op jit(solution)/shard_map/arrange/pallas_call | solution.py:173
  2.0 0.0 copy-start.3
  2.0 0.0 copy-start.2
  2.0 0.0 copy-start.1
  2.0 0.0 copy-start
  2.1 11.9 %all-to-all-start = ((f32[16,2,2,8,128]{4,3,2,1,0:T(8,128)}), f32[16,2,2,8,128]{4,3,2,1,0:T(8,128)S(1)}, u32[]{:S(2)}, u32[]{:S(2)}) async-start(f32[16,2,2,8,128]{4,3,2,1,0:T(8,128)} %get-tuple-element.19), calls=%async_computation | async-start | bytes 524288 | tf_op jit(solution)/shard_map/all_to_all | solution.py:182
  14.0 0.0 copy-done.3
  14.0 1.4 %collective-permute-start = (s32[2,8,1024]{2,1,0:T(8,128)S(1)}, s32[2,8,1024]{2,1,0:T(8,128)S(1)}, u32[]{:S(2)}, u32[]{:S(2)}) collective-permute-start(s32[2,8,1024]{2,1,0:T(8,128)S(1)} %copy-done.3), channel_id=1, source_target_pairs={{0,16},{16,0},{32,48},{48,32},{1,17},{17,1},{33,49},{49,33},{2,18}... | collective-permute-start | bytes 196616 | tf_op jit(solution)/shard_map/ppermute | solution.py:159
  15.4 0.0 copy-done.2
  15.4 2.4 %collective-permute-start.1 = (s32[2,8,1024]{2,1,0:T(8,128)S(1)}, s32[2,8,1024]{2,1,0:T(8,128)S(1)}, u32[]{:S(2)}, u32[]{:S(2)}) collective-permute-start(s32[2,8,1024]{2,1,0:T(8,128)S(1)} %copy-done.2), channel_id=1, source_target_pairs={{0,32},{16,48},{32,0},{48,16},{1,33},{17,49},{33,1},{49,17},{2,34}... | collective-permute-start | bytes 196616 | tf_op jit(solution)/shard_map/ppermute | solution.py:159
  17.8 0.0 copy-done.1
  17.8 0.1 collective-permute-start.2
  17.9 0.2 broadcast_subtract_fusion
  18.2 0.1 sub.64
  18.3 0.1 div.52
  18.3 0.1 div.53
  18.5 0.0 collective-permute-done
  18.5 2.6 %collective-permute-done.1 = s32[2,8,1024]{2,1,0:T(8,128)S(1)} collective-permute-done((s32[2,8,1024]{2,1,0:T(8,128)S(1)}, s32[2,8,1024]{2,1,0:T(8,128)S(1)}, u32[]{:S(2)}, u32[]{:S(2)}) %collective-permute-start.1) | collective-permute-done | bytes 65568 | tf_op jit(solution)/shard_map/ppermute | solution.py:159
  21.0 2.5 %collective-permute-done.2 = s32[2,8,1024]{2,1,0:T(8,128)S(1)} collective-permute-done((s32[2,8,1024]{2,1,0:T(8,128)S(1)}, s32[2,8,1024]{2,1,0:T(8,128)S(1)}, u32[]{:S(2)}, u32[]{:S(2)}) %collective-permute-start.2) | collective-permute-done | bytes 65568 | tf_op jit(solution)/shard_map/ppermute | solution.py:159
  23.5 0.0 copy-done
  23.5 1.5 %prepare.1 = (s32[8,128]{1,0:T(8,128)S(4)}, f32[4,8,8,8,128]{4,3,2,1,0:T(8,128)S(1)}, f32[4,8,8,8,128]{4,3,2,1,0:T(8,128)S(1)}, s32[4,8,8,8,128]{4,3,2,1,0:T(8,128)S(1)}) custom-call(f32[1,128]{1,0:T(1,128)S(1)} %fusion.30.refs_0_, s32[4,2,8,1024]{3,2,1,0:T(8,128)S(1)} %pad_add_fusion.refs_1_), custom_call_target="tpu_custom_call" | custom-call | flops 9830400 | bytes 3407872 | tf_op jit(solution)/shard_map/prepare/pallas_call | solution.py:185
  25.0 0.0 all-to-all-done.refs_1_
  25.0 0.7 %project.3 = f32[16,8,128]{2,1,0:T(8,128)S(1)} custom-call(s32[8,128]{1,0:T(8,128)S(4)} %get-tuple-element.18.refs_0_, f32[16,2,2,8,128]{4,3,2,1,0:T(8,128)S(1)} %all-to-all-done.refs_1_, f32[4,8,8,8,128]{4,3,2,1,0:T(8,128)S(1)} %get-tuple-element.20.refs_2_, f32[4,8,8,8,128]{4,3,2,1,0:T(8,128)S(1)} %get-tuple-element.21.refs_3_, ...), custom_call_target="tpu_custom_call" | custom-call | flops 16777216 | bytes 2097152 | tf_op jit(solution)/shard_map/project/pallas_call | solution.py:201
  25.8 2.6 %collective-permute-start.3 = (f32[16,8,128]{2,1,0:T(8,128)S(1)}, f32[16,8,128]{2,1,0:T(8,128)S(1)}, u32[]{:S(2)}, u32[]{:S(2)}) collective-permute-start(f32[16,8,128]{2,1,0:T(8,128)S(1)} %project.3), channel_id=1, source_target_pairs={{0,1},{1,0},{2,3},{3,2},{4,5},{5,4},{6,7},{7,6},{8,9},{9,8},{10,11... | collective-permute-start | bytes 196616 | tf_op jit(solution)/shard_map/ppermute | solution.py:211
  28.3 0.7 %project.2 = f32[16,8,128]{2,1,0:T(8,128)S(1)} custom-call(s32[8,128]{1,0:T(8,128)S(4)} %get-tuple-element.18.refs_0_, f32[16,2,2,8,128]{4,3,2,1,0:T(8,128)S(1)} %all-to-all-done.refs_1_, f32[4,8,8,8,128]{4,3,2,1,0:T(8,128)S(1)} %get-tuple-element.20.refs_2_, f32[4,8,8,8,128]{4,3,2,1,0:T(8,128)S(1)} %get-tuple-element.21.refs_3_, ...), custom_call_target="tpu_custom_call" | custom-call | flops 16777216 | bytes 2097152 | tf_op jit(solution)/shard_map/project/pallas_call | solution.py:201
  29.1 0.2 collective-permute-done.3
  29.3 12.9 %all_to_all.10 = f32[32,4,128]{2,1,0:T(4,128)S(1)} all-to-all(f32[32,4,128]{2,1,0:T(4,128)S(1)} %bitcast.5), channel_id=1, replica_groups=mesh['far'=4,'near'=4,'x'=4,'pair'=2,'core'=2] {'near','x','pair'}, dimensions={0} | all-to-all | bytes 131072 | tf_op jit(solution)/shard_map/all_to_all | solution.py:213
  42.2 0.6 %reshape.167 = f32[2,256]{1,0:T(2,128)} reshape(f32[4,128]{1,0:T(4,128)S(1)} %reduce_sum.19) | data formatting | bytes 4096 | tf_op jit(solution)/shard_map/reshape | solution.py:214
  (6 shorter events, 0.1 us)
Async XLA Ops:
  2.0 11.9 %copy-start.3 = (s32[2,8,1024]{2,1,0:T(8,128)S(1)}, s32[2,8,1024]{2,1,0:T(8,128)}, u32[]{:S(2)}) copy-start(s32[2,8,1024]{2,1,0:T(8,128)} %get-tuple-element.15) | copy-start | bytes 196612
  2.0 13.4 %copy-start.2 = (s32[2,8,1024]{2,1,0:T(8,128)S(1)}, s32[2,8,1024]{2,1,0:T(8,128)}, u32[]{:S(2)}) copy-start(s32[2,8,1024]{2,1,0:T(8,128)} %get-tuple-element.16) | copy-start | bytes 196612
  2.0 15.8 %copy-start.1 = (s32[2,8,1024]{2,1,0:T(8,128)S(1)}, s32[2,8,1024]{2,1,0:T(8,128)}, u32[]{:S(2)}) copy-start(s32[2,8,1024]{2,1,0:T(8,128)} %get-tuple-element.17) | copy-start | bytes 196612
  2.0 21.5 %copy-start = (s32[2,8,1024]{2,1,0:T(8,128)S(1)}, s32[2,8,1024]{2,1,0:T(8,128)}, u32[]{:S(2)}) copy-start(s32[2,8,1024]{2,1,0:T(8,128)} %get-tuple-element.14) | copy-start | bytes 196612
  2.1 23.0 %all-to-all-start = ((f32[16,2,2,8,128]{4,3,2,1,0:T(8,128)}), f32[16,2,2,8,128]{4,3,2,1,0:T(8,128)S(1)}, u32[]{:S(2)}, u32[]{:S(2)}) async-start(f32[16,2,2,8,128]{4,3,2,1,0:T(8,128)} %get-tuple-element.19), calls=%async_computation | async-start | bytes 524288 | tf_op jit(solution)/shard_map/all_to_all | solution.py:182
  14.0 4.5 %collective-permute-start = (s32[2,8,1024]{2,1,0:T(8,128)S(1)}, s32[2,8,1024]{2,1,0:T(8,128)S(1)}, u32[]{:S(2)}, u32[]{:S(2)}) collective-permute-start(s32[2,8,1024]{2,1,0:T(8,128)S(1)} %copy-done.3), channel_id=1, source_target_pairs={{0,16},{16,0},{32,48},{48,32},{1,17},{17,1},{33,49},{49,33},{2,18}... | collective-permute-start | bytes 196616 | tf_op jit(solution)/shard_map/ppermute | solution.py:159
  15.4 5.6 %collective-permute-start.1 = (s32[2,8,1024]{2,1,0:T(8,128)S(1)}, s32[2,8,1024]{2,1,0:T(8,128)S(1)}, u32[]{:S(2)}, u32[]{:S(2)}) collective-permute-start(s32[2,8,1024]{2,1,0:T(8,128)S(1)} %copy-done.2), channel_id=1, source_target_pairs={{0,32},{16,48},{32,0},{48,16},{1,33},{17,49},{33,1},{49,17},{2,34}... | collective-permute-start | bytes 196616 | tf_op jit(solution)/shard_map/ppermute | solution.py:159
  17.8 5.7 %collective-permute-start.2 = (s32[2,8,1024]{2,1,0:T(8,128)S(1)}, s32[2,8,1024]{2,1,0:T(8,128)S(1)}, u32[]{:S(2)}, u32[]{:S(2)}) collective-permute-start(s32[2,8,1024]{2,1,0:T(8,128)S(1)} %copy-done.1), channel_id=1, source_target_pairs={{0,48},{16,32},{32,16},{48,0},{1,49},{17,33},{33,17},{49,1},{2,50}... | collective-permute-start | bytes 196616 | tf_op jit(solution)/shard_map/ppermute | solution.py:159
  25.8 3.5 %collective-permute-start.3 = (f32[16,8,128]{2,1,0:T(8,128)S(1)}, f32[16,8,128]{2,1,0:T(8,128)S(1)}, u32[]{:S(2)}, u32[]{:S(2)}) collective-permute-start(f32[16,8,128]{2,1,0:T(8,128)S(1)} %project.3), channel_id=1, source_target_pairs={{0,1},{1,0},{2,3},{3,2},{4,5},{5,4},{6,7},{7,6},{8,9},{9,8},{10,11... | collective-permute-start | bytes 196616 | tf_op jit(solution)/shard_map/ppermute | solution.py:211

commit v5 on v4

--- a/solution.py
+++ b/solution.py
@@ -177,8 +177,9 @@
         in_specs=[vmem] * 3,
         out_specs=[vmem] * (SIDE + 1),
         scratch_shapes=[pltpu.VMEM((2, pulses, TAPS, bins // TAPS), jnp.float32)],
+        compiler_params=pltpu.CompilerParams(vmem_limit_bytes=4 << 20),
         name="arrange",
-    )(profile, base_bin, tap_offset)
+    )(*(pltpu.with_memory_space_constraint(value, pltpu.HBM) for value in (profile, base_bin, tap_offset)))
     whole = lax.all_to_all(shards, ("far", "near"), 0, 0, tiled=True)
     index = jnp.stack([index[0]] + [swap(index[step], step) for step in range(1, SIDE)])
     by_part = (SIDE, SUBLANES, parts, TAPS, LANES)

time: 43.1 us -> 42.9 us (level)
  no operation moved by 1% of the time
where the time goes in v5:
time: 42.9 us; the launch traced here: 42.6 us
  starting transfers between devices  18.3 us (43%)
  blocking collectives  12.9 us (30%)
  waiting for transfers between devices  5.24 us (12%)
  Pallas kernels  4.91 us (11%)
  local copies, waits for them, and re-layouts  0.85 us (2%)
    all_to_all x1, blocking collectives, local(): lax.all_to_all(partial_image, ('near', 'x', 'pair'), 0, 0, tiled=True)  12.9 us
    all_to_all x1, starting transfers between devices, local(): whole = lax.all_to_all(shards, ('far', 'near'), 0, 0, tiled=True)  11.7 us
    ppermute x3, waiting for transfers between devices, swap(): return lax.ppermute(value, 'near', [(i, i ^ step) for i in range(SIDE)])  5.05 us
    ppermute x3, starting transfers between devices, swap(): return lax.ppermute(value, 'near', [(i, i ^ step) for i in range(SIDE)])  3.95 us
    ppermute x1, starting transfers between devices, local(): theirs = lax.ppermute(project(False), 'core', [(0, 1), (1, 0)])  2.58 us
    pallas_call x1, Pallas kernels, local(): pl.pallas_call(arrange_kernel, out_shape=[jax.ShapeDtypeStruct((2, SUBLAN...  2.01 us
    pallas_call x1, Pallas kernels, local(): pl.pallas_call(lambda *refs: prepare_kernel(scale, *refs), out_shape=[plt...  1.47 us
    pallas_call x2, Pallas kernels, project(): pl.pallas_call(lambda *refs: project_kernel(own, *refs), out_shape=jax.Sh...  1.43 us
  transfers between devices with their start and end apart: 5, of which 3 were waited for; matrix products, arithmetic and copies ran while one was open for 1% of the time, Pallas kernels for 5%

profile of v5, /device:TPU:1, one launch (start us, length us, event | category | flops | bytes accessed | tf_op | source)
XLA Modules:
  0.0 42.6 jit_solution(330138072071821845)
XLA Ops:
  0.0 2.0 %arrange.1 = (s32[2,8,1024]{2,1,0:T(8,128)S(1)}, s32[2,8,1024]{2,1,0:T(8,128)S(1)}, s32[2,8,1024]{2,1,0:T(8,128)S(1)}, s32[2,8,1024]{2,1,0:T(8,128)S(1)}, f32[16,2,2,8,128]{4,3,2,1,0:T(8,128)}) custom-call(f32[2,8,1024]{2,1,0:T(8,128)} %shard_ref.1, s32[8,4096]{1,0:T(8,128)} %bins_ref.1, s32[8,4096]{1,0:T(8,128)} %offsets_ref.1), custom_call_target="tpu_custom_call" | custom-call | tf_op jit(solution)/shard_map/arrange/pallas_call | solution.py:173
  2.0 11.7 %all-to-all-start = ((f32[16,2,2,8,128]{4,3,2,1,0:T(8,128)}), f32[16,2,2,8,128]{4,3,2,1,0:T(8,128)S(1)}, u32[]{:S(2)}, u32[]{:S(2)}) async-start(f32[16,2,2,8,128]{4,3,2,1,0:T(8,128)} %get-tuple-element.19), calls=%async_computation | async-start | bytes 524288 | tf_op jit(solution)/shard_map/all_to_all | solution.py:183
  13.8 1.4 %collective-permute-start = (s32[2,8,1024]{2,1,0:T(8,128)S(1)}, s32[2,8,1024]{2,1,0:T(8,128)S(1)}, u32[]{:S(2)}, u32[]{:S(2)}) collective-permute-start(s32[2,8,1024]{2,1,0:T(8,128)S(1)} %get-tuple-element.15), channel_id=1, source_target_pairs={{0,16},{16,0},{32,48},{48,32},{1,17},{17,1},{33,49},{49,33},{2,18}... | collective-permute-start | bytes 196616 | tf_op jit(solution)/shard_map/ppermute | solution.py:159
  15.1 2.4 %collective-permute-start.1 = (s32[2,8,1024]{2,1,0:T(8,128)S(1)}, s32[2,8,1024]{2,1,0:T(8,128)S(1)}, u32[]{:S(2)}, u32[]{:S(2)}) collective-permute-start(s32[2,8,1024]{2,1,0:T(8,128)S(1)} %get-tuple-element.16), channel_id=1, source_target_pairs={{0,32},{16,48},{32,0},{48,16},{1,33},{17,49},{33,1},{49,17},{2,34}... | collective-permute-start | bytes 196616 | tf_op jit(solution)/shard_map/ppermute | solution.py:159
  17.5 0.2 collective-permute-start.2
  17.7 0.2 broadcast_subtract_fusion
  18.0 0.1 sub.64
  18.1 0.1 div.52
  18.1 0.1 div.53
  18.3 0.0 collective-permute-done
  18.3 2.6 %collective-permute-done.1 = s32[2,8,1024]{2,1,0:T(8,128)S(1)} collective-permute-done((s32[2,8,1024]{2,1,0:T(8,128)S(1)}, s32[2,8,1024]{2,1,0:T(8,128)S(1)}, u32[]{:S(2)}, u32[]{:S(2)}) %collective-permute-start.1) | collective-permute-done | bytes 65568 | tf_op jit(solution)/shard_map/ppermute | solution.py:159
  20.9 2.5 %collective-permute-done.2 = s32[2,8,1024]{2,1,0:T(8,128)S(1)} collective-permute-done((s32[2,8,1024]{2,1,0:T(8,128)S(1)}, s32[2,8,1024]{2,1,0:T(8,128)S(1)}, u32[]{:S(2)}, u32[]{:S(2)}) %collective-permute-start.2) | collective-permute-done | bytes 65568 | tf_op jit(solution)/shard_map/ppermute | solution.py:159
  23.4 1.5 %prepare.1 = (s32[8,128]{1,0:T(8,128)S(4)}, f32[4,8,8,8,128]{4,3,2,1,0:T(8,128)S(1)}, f32[4,8,8,8,128]{4,3,2,1,0:T(8,128)S(1)}, s32[4,8,8,8,128]{4,3,2,1,0:T(8,128)S(1)}) custom-call(f32[1,128]{1,0:T(1,128)S(1)} %fusion.30.refs_0_, s32[4,2,8,1024]{3,2,1,0:T(8,128)S(1)} %pad_add_fusion.refs_1_), custom_call_target="tpu_custom_call" | custom-call | flops 9830400 | bytes 3407872 | tf_op jit(solution)/shard_map/prepare/pallas_call | solution.py:186
  24.8 0.0 all-to-all-done.refs_1_
  24.8 0.7 %project.3 = f32[16,8,128]{2,1,0:T(8,128)S(1)} custom-call(s32[8,128]{1,0:T(8,128)S(4)} %get-tuple-element.18.refs_0_, f32[16,2,2,8,128]{4,3,2,1,0:T(8,128)S(1)} %all-to-all-done.refs_1_, f32[4,8,8,8,128]{4,3,2,1,0:T(8,128)S(1)} %get-tuple-element.20.refs_2_, f32[4,8,8,8,128]{4,3,2,1,0:T(8,128)S(1)} %get-tuple-element.21.refs_3_, ...), custom_call_target="tpu_custom_call" | custom-call | flops 16777216 | bytes 2097152 | tf_op jit(solution)/shard_map/project/pallas_call | solution.py:202
  25.6 2.6 %collective-permute-start.3 = (f32[16,8,128]{2,1,0:T(8,128)S(1)}, f32[16,8,128]{2,1,0:T(8,128)S(1)}, u32[]{:S(2)}, u32[]{:S(2)}) collective-permute-start(f32[16,8,128]{2,1,0:T(8,128)S(1)} %project.3), channel_id=1, source_target_pairs={{0,1},{1,0},{2,3},{3,2},{4,5},{5,4},{6,7},{7,6},{8,9},{9,8},{10,11... | collective-permute-start | bytes 196616 | tf_op jit(solution)/shard_map/ppermute | solution.py:212
  28.1 0.7 %project.2 = f32[16,8,128]{2,1,0:T(8,128)S(1)} custom-call(s32[8,128]{1,0:T(8,128)S(4)} %get-tuple-element.18.refs_0_, f32[16,2,2,8,128]{4,3,2,1,0:T(8,128)S(1)} %all-to-all-done.refs_1_, f32[4,8,8,8,128]{4,3,2,1,0:T(8,128)S(1)} %get-tuple-element.20.refs_2_, f32[4,8,8,8,128]{4,3,2,1,0:T(8,128)S(1)} %get-tuple-element.21.refs_3_, ...), custom_call_target="tpu_custom_call" | custom-call | flops 16777216 | bytes 2097152 | tf_op jit(solution)/shard_map/project/pallas_call | solution.py:202
  28.9 0.2 collective-permute-done.3
  29.1 12.9 %all_to_all.10 = f32[32,4,128]{2,1,0:T(4,128)S(1)} all-to-all(f32[32,4,128]{2,1,0:T(4,128)S(1)} %bitcast.6), channel_id=1, replica_groups=mesh['far'=4,'near'=4,'x'=4,'pair'=2,'core'=2] {'near','x','pair'}, dimensions={0} | all-to-all | bytes 131072 | tf_op jit(solution)/shard_map/all_to_all | solution.py:214
  42.0 0.6 %reshape.167 = f32[2,256]{1,0:T(2,128)} reshape(f32[4,128]{1,0:T(4,128)S(1)} %reduce_sum.19) | data formatting | bytes 4096 | tf_op jit(solution)/shard_map/reshape | solution.py:215
  (6 shorter events, 0.1 us)
Async XLA Ops:
  2.0 22.8 %all-to-all-start = ((f32[16,2,2,8,128]{4,3,2,1,0:T(8,128)}), f32[16,2,2,8,128]{4,3,2,1,0:T(8,128)S(1)}, u32[]{:S(2)}, u32[]{:S(2)}) async-start(f32[16,2,2,8,128]{4,3,2,1,0:T(8,128)} %get-tuple-element.19), calls=%async_computation | async-start | bytes 524288 | tf_op jit(solution)/shard_map/all_to_all | solution.py:183
  13.8 4.5 %collective-permute-start = (s32[2,8,1024]{2,1,0:T(8,128)S(1)}, s32[2,8,1024]{2,1,0:T(8,128)S(1)}, u32[]{:S(2)}, u32[]{:S(2)}) collective-permute-start(s32[2,8,1024]{2,1,0:T(8,128)S(1)} %get-tuple-element.15), channel_id=1, source_target_pairs={{0,16},{16,0},{32,48},{48,32},{1,17},{17,1},{33,49},{49,33},{2,18}... | collective-permute-start | bytes 196616 | tf_op jit(solution)/shard_map/ppermute | solution.py:159
  15.1 5.7 %collective-permute-start.1 = (s32[2,8,1024]{2,1,0:T(8,128)S(1)}, s32[2,8,1024]{2,1,0:T(8,128)S(1)}, u32[]{:S(2)}, u32[]{:S(2)}) collective-permute-start(s32[2,8,1024]{2,1,0:T(8,128)S(1)} %get-tuple-element.16), channel_id=1, source_target_pairs={{0,32},{16,48},{32,0},{48,16},{1,33},{17,49},{33,1},{49,17},{2,34}... | collective-permute-start | bytes 196616 | tf_op jit(solution)/shard_map/ppermute | solution.py:159
  17.5 5.8 %collective-permute-start.2 = (s32[2,8,1024]{2,1,0:T(8,128)S(1)}, s32[2,8,1024]{2,1,0:T(8,128)S(1)}, u32[]{:S(2)}, u32[]{:S(2)}) collective-permute-start(s32[2,8,1024]{2,1,0:T(8,128)S(1)} %get-tuple-element.17), channel_id=1, source_target_pairs={{0,48},{16,32},{32,16},{48,0},{1,49},{17,33},{33,17},{49,1},{2,50}... | collective-permute-start | bytes 196616 | tf_op jit(solution)/shard_map/ppermute | solution.py:159
  25.6 3.5 %collective-permute-start.3 = (f32[16,8,128]{2,1,0:T(8,128)S(1)}, f32[16,8,128]{2,1,0:T(8,128)S(1)}, u32[]{:S(2)}, u32[]{:S(2)}) collective-permute-start(f32[16,8,128]{2,1,0:T(8,128)S(1)} %project.3), channel_id=1, source_target_pairs={{0,1},{1,0},{2,3},{3,2},{4,5},{5,4},{6,7},{7,6},{8,9},{9,8},{10,11... | collective-permute-start | bytes 196616 | tf_op jit(solution)/shard_map/ppermute | solution.py:212

commit v6 on v5

--- a/solution.py
+++ b/solution.py
@@ -77,7 +77,7 @@
             for p in range(each):
                 tile = tiles[c, place * each + p]
                 for far in range(SIDE):
-                    out_ref[far * SIDE + place, c, p] = tile
+                    out_ref[SIDE * SIDE - 1 - (far * SIDE + place), c, p] = tile
 
 
 def prepare_kernel(scale, table_ref, index_ref, first_ref, real_ref, imag_ref, lane_ref, lowest_ref, sem):
@@ -143,7 +143,7 @@
                     owner = first >> 10
                     after = jnp.minimum(owner + 1, owners - 1)
                     here = column >= ((first >> 3) & (LANES - 1))
-                    table = [jnp.where(here, whole[owner, c, p], whole[after, c, p]) for c in range(2)]
+                    table = [jnp.where(here, whole[owners - 1 - owner, c, p], whole[owners - 1 - after, c, p]) for c in range(2)]
                     for half in range(halves):
                         part = block * halves + half
                         lane = lane_ref[tile, row, part]
@@ -151,12 +151,16 @@
                         real, imag = real_ref[tile, row, part], imag_ref[tile, row, part]
                         total[0][half] = total[0][half] + (got[0] * real - got[1] * imag)
                         total[1][half] = total[1][half] + (got[0] * imag + got[1] * real)
-                sums += total[0] + total[1]
-            out_ref[(tile ^ near) * quarters + quarter] = row_sums(sums)
+                sums = total[0] + total[1] + sums
+            out_ref[tiles * quarters - 1 - ((tile ^ near) * quarters + quarter)] = row_sums(sums)
 
 
 def swap(value, step):
     return lax.ppermute(value, "near", [(i, i ^ step) for i in range(SIDE)])
+
+
+def backward(value, axes):
+    return lax.all_to_all(value, axes, 0, 0, tiled=True, axis_index_groups=[list(range(value.shape[0]))[::-1]])
 
 
 def local(profile, base_bin, tap_offset):
@@ -180,7 +184,7 @@
         compiler_params=pltpu.CompilerParams(vmem_limit_bytes=4 << 20),
         name="arrange",
     )(*(pltpu.with_memory_space_constraint(value, pltpu.HBM) for value in (profile, base_bin, tap_offset)))
-    whole = lax.all_to_all(shards, ("far", "near"), 0, 0, tiled=True)
+    whole = backward(shards, ("far", "near"))
     index = jnp.stack([index[0]] + [swap(index[step], step) for step in range(1, SIDE)])
     by_part = (SIDE, SUBLANES, parts, TAPS, LANES)
     first, real, imag, lane = pl.pallas_call(
@@ -211,7 +215,7 @@
 
     theirs = lax.ppermute(project(False), "core", [(0, 1), (1, 0)])
     partial_image = (project(True) + theirs).reshape(SIDE * pixels // BLOCK // 2, 2 * BLOCK // LANES, LANES)
-    received = lax.all_to_all(partial_image, ("near", "x", "pair"), 0, 0, tiled=True)
+    received = backward(partial_image, ("near", "x", "pair"))
     return jnp.sum(received, axis=0).reshape(2, BLOCK)
 
 

time: 42.9 us -> 39.9 us (0.930)
  blocking collectives: 12.9 us -> 11.3 us
  starting transfers between devices: 18.3 us -> 17.4 us
  waiting for transfers between devices: 5.24 us -> 4.71 us
    ppermute x1, starting transfers between devices: 2.58 us -> 0.82 us  [local(): theirs = lax.ppermute(project(False), 'core', [(0, 1), (1, 0)])]
    all_to_all x1, blocking collectives: 12.9 us -> 11.3 us  [backward(): lax.all_to_all(value, axes, 0, 0, tiled=True, axis_index_groups=[list(ran...]
    all_to_all x1, starting transfers between devices: 11.7 us -> 12.7 us  [backward(): lax.all_to_all(value, axes, 0, 0, tiled=True, axis_index_groups=[list(ran...]
    ppermute x3, waiting for transfers between devices: 5.05 us -> 4.53 us  [swap(): return lax.ppermute(value, 'near', [(i, i ^ step) for i in range(SIDE)])]
  transfers between devices with their start and end apart: 5 -> 5, of which waited for: 3 -> 3; matrix products, arithmetic and copies ran while one was open for 1% -> 1% of each run, Pallas kernels for 5% -> 6%
where the time goes in v6:
time: 39.9 us; the launch traced here: 39.6 us
  starting transfers between devices  17.4 us (44%)
  blocking collectives  11.3 us (28%)
  Pallas kernels  4.91 us (12%)
  waiting for transfers between devices  4.71 us (12%)
  local copies, waits for them, and re-layouts  0.85 us (2%)
    all_to_all x1, starting transfers between devices, backward(): lax.all_to_all(value, axes, 0, 0, tiled=True, axis_index_groups=[list(ran...  12.7 us
    all_to_all x1, blocking collectives, backward(): lax.all_to_all(value, axes, 0, 0, tiled=True, axis_index_groups=[list(ran...  11.3 us
    ppermute x3, waiting for transfers between devices, swap(): return lax.ppermute(value, 'near', [(i, i ^ step) for i in range(SIDE)])  4.53 us
    ppermute x3, starting transfers between devices, swap(): return lax.ppermute(value, 'near', [(i, i ^ step) for i in range(SIDE)])  3.86 us
    pallas_call x1, Pallas kernels, local(): pl.pallas_call(arrange_kernel, out_shape=[jax.ShapeDtypeStruct((2, SUBLAN...  2.01 us
    pallas_call x1, Pallas kernels, local(): pl.pallas_call(lambda *refs: prepare_kernel(scale, *refs), out_shape=[plt...  1.47 us
    pallas_call x2, Pallas kernels, project(): pl.pallas_call(lambda *refs: project_kernel(own, *refs), out_shape=jax.Sh...  1.43 us
    ppermute x1, starting transfers between devices, local(): theirs = lax.ppermute(project(False), 'core', [(0, 1), (1, 0)])  0.82 us
  transfers between devices with their start and end apart: 5, of which 3 were waited for; matrix products, arithmetic and copies ran while one was open for 1% of the time, Pallas kernels for 6%

profile of v6, /device:TPU:1, one launch (start us, length us, event | category | flops | bytes accessed | tf_op | source)
XLA Modules:
  0.0 39.6 jit_solution(10015661130597353671)
XLA Ops:
  0.0 2.0 %arrange.1 = (s32[2,8,1024]{2,1,0:T(8,128)S(1)}, s32[2,8,1024]{2,1,0:T(8,128)S(1)}, s32[2,8,1024]{2,1,0:T(8,128)S(1)}, s32[2,8,1024]{2,1,0:T(8,128)S(1)}, f32[16,2,2,8,128]{4,3,2,1,0:T(8,128)}) custom-call(f32[2,8,1024]{2,1,0:T(8,128)} %shard_ref.1, s32[8,4096]{1,0:T(8,128)} %bins_ref.1, s32[8,4096]{1,0:T(8,128)} %offsets_ref.1), custom_call_target="tpu_custom_call" | custom-call | tf_op jit(solution)/shard_map/arrange/pallas_call | solution.py:177
  2.0 12.7 %all-to-all-start = ((f32[16,2,2,8,128]{4,3,2,1,0:T(8,128)}), f32[16,2,2,8,128]{4,3,2,1,0:T(8,128)S(1)}, u32[]{:S(2)}, u32[]{:S(2)}) async-start(f32[16,2,2,8,128]{4,3,2,1,0:T(8,128)} %get-tuple-element.19), calls=%async_computation | async-start | bytes 524288 | tf_op jit(solution)/shard_map/all_to_all | solution.py:163
  14.7 0.6 %collective-permute-start = (s32[2,8,1024]{2,1,0:T(8,128)S(1)}, s32[2,8,1024]{2,1,0:T(8,128)S(1)}, u32[]{:S(2)}, u32[]{:S(2)}) collective-permute-start(s32[2,8,1024]{2,1,0:T(8,128)S(1)} %get-tuple-element.15), channel_id=1, source_target_pairs={{0,16},{16,0},{32,48},{48,32},{1,17},{17,1},{33,49},{49,33},{2,18}... | collective-permute-start | bytes 196616 | tf_op jit(solution)/shard_map/ppermute | solution.py:159
  15.3 0.9 %collective-permute-start.1 = (s32[2,8,1024]{2,1,0:T(8,128)S(1)}, s32[2,8,1024]{2,1,0:T(8,128)S(1)}, u32[]{:S(2)}, u32[]{:S(2)}) collective-permute-start(s32[2,8,1024]{2,1,0:T(8,128)S(1)} %get-tuple-element.16), channel_id=1, source_target_pairs={{0,32},{16,48},{32,0},{48,16},{1,33},{17,49},{33,1},{49,17},{2,34}... | collective-permute-start | bytes 196616 | tf_op jit(solution)/shard_map/ppermute | solution.py:159
  16.2 2.4 %collective-permute-start.2 = (s32[2,8,1024]{2,1,0:T(8,128)S(1)}, s32[2,8,1024]{2,1,0:T(8,128)S(1)}, u32[]{:S(2)}, u32[]{:S(2)}) collective-permute-start(s32[2,8,1024]{2,1,0:T(8,128)S(1)} %get-tuple-element.17), channel_id=1, source_target_pairs={{0,48},{16,32},{32,16},{48,0},{1,49},{17,33},{33,17},{49,1},{2,50}... | collective-permute-start | bytes 196616 | tf_op jit(solution)/shard_map/ppermute | solution.py:159
  18.6 0.2 broadcast_subtract_fusion
  18.8 0.1 sub.64
  18.9 0.1 div.52
  19.0 0.1 div.53
  19.1 0.0 collective-permute-done
  19.2 3.0 %collective-permute-done.1 = s32[2,8,1024]{2,1,0:T(8,128)S(1)} collective-permute-done((s32[2,8,1024]{2,1,0:T(8,128)S(1)}, s32[2,8,1024]{2,1,0:T(8,128)S(1)}, u32[]{:S(2)}, u32[]{:S(2)}) %collective-permute-start.1) | collective-permute-done | bytes 65568 | tf_op jit(solution)/shard_map/ppermute | solution.py:159
  22.1 1.5 %collective-permute-done.2 = s32[2,8,1024]{2,1,0:T(8,128)S(1)} collective-permute-done((s32[2,8,1024]{2,1,0:T(8,128)S(1)}, s32[2,8,1024]{2,1,0:T(8,128)S(1)}, u32[]{:S(2)}, u32[]{:S(2)}) %collective-permute-start.2) | collective-permute-done | bytes 65568 | tf_op jit(solution)/shard_map/ppermute | solution.py:159
  23.7 1.5 %prepare.1 = (s32[8,128]{1,0:T(8,128)S(4)}, f32[4,8,8,8,128]{4,3,2,1,0:T(8,128)S(1)}, f32[4,8,8,8,128]{4,3,2,1,0:T(8,128)S(1)}, s32[4,8,8,8,128]{4,3,2,1,0:T(8,128)S(1)}) custom-call(f32[1,128]{1,0:T(1,128)S(1)} %fusion.30.refs_0_, s32[4,2,8,1024]{3,2,1,0:T(8,128)S(1)} %pad_add_fusion.refs_1_), custom_call_target="tpu_custom_call" | custom-call | flops 9830400 | bytes 3407872 | tf_op jit(solution)/shard_map/prepare/pallas_call | solution.py:190
  25.2 0.0 all-to-all-done.refs_1_
  25.2 0.7 %project.3 = f32[16,8,128]{2,1,0:T(8,128)S(1)} custom-call(s32[8,128]{1,0:T(8,128)S(4)} %get-tuple-element.18.refs_0_, f32[16,2,2,8,128]{4,3,2,1,0:T(8,128)S(1)} %all-to-all-done.refs_1_, f32[4,8,8,8,128]{4,3,2,1,0:T(8,128)S(1)} %get-tuple-element.20.refs_2_, f32[4,8,8,8,128]{4,3,2,1,0:T(8,128)S(1)} %get-tuple-element.21.refs_3_, ...), custom_call_target="tpu_custom_call" | custom-call | flops 16777216 | bytes 2097152 | tf_op jit(solution)/shard_map/project/pallas_call | solution.py:206
  25.9 0.8 %collective-permute-start.3 = (f32[16,8,128]{2,1,0:T(8,128)S(1)}, f32[16,8,128]{2,1,0:T(8,128)S(1)}, u32[]{:S(2)}, u32[]{:S(2)}) collective-permute-start(f32[16,8,128]{2,1,0:T(8,128)S(1)} %project.3), channel_id=1, source_target_pairs={{0,1},{1,0},{2,3},{3,2},{4,5},{5,4},{6,7},{7,6},{8,9},{9,8},{10,11... | collective-permute-start | bytes 196616 | tf_op jit(solution)/shard_map/ppermute | solution.py:216
  26.7 0.7 %project.2 = f32[16,8,128]{2,1,0:T(8,128)S(1)} custom-call(s32[8,128]{1,0:T(8,128)S(4)} %get-tuple-element.18.refs_0_, f32[16,2,2,8,128]{4,3,2,1,0:T(8,128)S(1)} %all-to-all-done.refs_1_, f32[4,8,8,8,128]{4,3,2,1,0:T(8,128)S(1)} %get-tuple-element.20.refs_2_, f32[4,8,8,8,128]{4,3,2,1,0:T(8,128)S(1)} %get-tuple-element.21.refs_3_, ...), custom_call_target="tpu_custom_call" | custom-call | flops 16777216 | bytes 2097152 | tf_op jit(solution)/shard_map/project/pallas_call | solution.py:206
  27.5 0.2 collective-permute-done.3
  27.7 11.3 %all_to_all.10 = f32[32,4,128]{2,1,0:T(4,128)S(1)} all-to-all(f32[32,4,128]{2,1,0:T(4,128)S(1)} %bitcast.6), channel_id=1, replica_groups={{62,60,58,56,54,52,50,48,46,44,42,40,38,36,34,32,30,28,26,24,22,20,18,1..., dimensions={0} | all-to-all | bytes 131072 | tf_op jit(solution)/shard_map/all_to_all | solution.py:163
  39.0 0.6 %reshape.167 = f32[2,256]{1,0:T(2,128)} reshape(f32[4,128]{1,0:T(4,128)S(1)} %reduce_sum.19) | data formatting | bytes 4096 | tf_op jit(solution)/shard_map/reshape | solution.py:219
  (6 shorter events, 0.1 us)
Async XLA Ops:
  2.0 23.2 %all-to-all-start = ((f32[16,2,2,8,128]{4,3,2,1,0:T(8,128)}), f32[16,2,2,8,128]{4,3,2,1,0:T(8,128)S(1)}, u32[]{:S(2)}, u32[]{:S(2)}) async-start(f32[16,2,2,8,128]{4,3,2,1,0:T(8,128)} %get-tuple-element.19), calls=%async_computation | async-start | bytes 524288 | tf_op jit(solution)/shard_map/all_to_all | solution.py:163
  14.7 4.4 %collective-permute-start = (s32[2,8,1024]{2,1,0:T(8,128)S(1)}, s32[2,8,1024]{2,1,0:T(8,128)S(1)}, u32[]{:S(2)}, u32[]{:S(2)}) collective-permute-start(s32[2,8,1024]{2,1,0:T(8,128)S(1)} %get-tuple-element.15), channel_id=1, source_target_pairs={{0,16},{16,0},{32,48},{48,32},{1,17},{17,1},{33,49},{49,33},{2,18}... | collective-permute-start | bytes 196616 | tf_op jit(solution)/shard_map/ppermute | solution.py:159
  15.3 6.8 %collective-permute-start.1 = (s32[2,8,1024]{2,1,0:T(8,128)S(1)}, s32[2,8,1024]{2,1,0:T(8,128)S(1)}, u32[]{:S(2)}, u32[]{:S(2)}) collective-permute-start(s32[2,8,1024]{2,1,0:T(8,128)S(1)} %get-tuple-element.16), channel_id=1, source_target_pairs={{0,32},{16,48},{32,0},{48,16},{1,33},{17,49},{33,1},{49,17},{2,34}... | collective-permute-start | bytes 196616 | tf_op jit(solution)/shard_map/ppermute | solution.py:159
  16.2 7.5 %collective-permute-start.2 = (s32[2,8,1024]{2,1,0:T(8,128)S(1)}, s32[2,8,1024]{2,1,0:T(8,128)S(1)}, u32[]{:S(2)}, u32[]{:S(2)}) collective-permute-start(s32[2,8,1024]{2,1,0:T(8,128)S(1)} %get-tuple-element.17), channel_id=1, source_target_pairs={{0,48},{16,32},{32,16},{48,0},{1,49},{17,33},{33,17},{49,1},{2,50}... | collective-permute-start | bytes 196616 | tf_op jit(solution)/shard_map/ppermute | solution.py:159
  25.9 1.7 %collective-permute-start.3 = (f32[16,8,128]{2,1,0:T(8,128)S(1)}, f32[16,8,128]{2,1,0:T(8,128)S(1)}, u32[]{:S(2)}, u32[]{:S(2)}) collective-permute-start(f32[16,8,128]{2,1,0:T(8,128)S(1)} %project.3), channel_id=1, source_target_pairs={{0,1},{1,0},{2,3},{3,2},{4,5},{5,4},{6,7},{7,6},{8,9},{9,8},{10,11... | collective-permute-start | bytes 196616 | tf_op jit(solution)/shard_map/ppermute | solution.py:216

commit v7 on v6

--- a/solution.py
+++ b/solution.py
@@ -14,6 +14,7 @@
 LANES = 128
 SUBLANES = 8
 SIDE = 4
+STEPS = (0, 3, 2, 1)
 AXES = ("far", "near", "x", "pair", "core")
 SIZES = (4, 4, 4, 2, 2)
 
@@ -80,34 +81,48 @@
                     out_ref[SIDE * SIDE - 1 - (far * SIDE + place), c, p] = tile
 
 
-def prepare_kernel(scale, table_ref, index_ref, first_ref, real_ref, imag_ref, lane_ref, lowest_ref, sem):
-    tiles, _, rows, length = index_ref.shape
-    halves = BLOCK // LANES
+def first_bins(index_ref):
+    _, rows, length = index_ref.shape
+    column = lax.broadcasted_iota(jnp.int32, (rows, LANES), 1)
+    firsts = jnp.zeros((rows, LANES), jnp.int32)
+    for block in range(length // BLOCK):
+        bins = index_ref[0, :, block * BLOCK : (block + 1) * BLOCK].astype(jnp.float32)
+        lowest = jnp.min(jnp.minimum(bins[:, :LANES], bins[:, LANES:]), axis=1, keepdims=True)
+        firsts = jnp.where(column == block, lowest.astype(jnp.int32), firsts)
+    return firsts
+
+
+def prepare_kernel(scale, table_ref, index_ref, *refs):
+    *before, first_ref, real_ref, imag_ref, lane_ref = refs[:-2] if len(refs) > 4 else refs
+    _, rows, length = index_ref.shape
+    firsts = first_bins(index_ref)
+    if before:
+        gathered_ref, sem = refs[-2:]
+        for tile, firsts_ref in enumerate(before):
+            mine = firsts_ref[:, :]
+            shift = tile * (length // BLOCK)
+            gathered = mine if tile == 0 else gathered + pltpu.roll(mine, shift, 1)
+        gathered_ref[:, :] = gathered + pltpu.roll(firsts, len(before) * (length // BLOCK), 1)
+        copy = pltpu.make_async_copy(gathered_ref, first_ref, sem)
+        copy.start()
+    else:
+        first_ref[:, :] = firsts
     table = spread(table_ref[:, :])
     phase = lax.broadcasted_iota(jnp.int32, (SUBLANES, LANES), 0)
-    lowest_ref[:, :] = jnp.zeros(lowest_ref.shape, jnp.int32)
-    for tile in range(tiles):
-        for block in range(length // BLOCK):
-            pair = [index_ref[tile, 0, :, (block * halves + h) * LANES : (block * halves + h + 1) * LANES] for h in range(halves)]
-            lowest = jnp.min(jnp.minimum(*pair).astype(jnp.float32), axis=1, keepdims=True)
-            count = tile * (length // BLOCK) + block
-            lowest_ref[:, count : count + 1] = lowest.astype(jnp.int32)
-    copy = pltpu.make_async_copy(lowest_ref, first_ref, sem)
-    copy.start()
-    for tile in range(tiles):
-        for part in range(length // LANES):
-            lanes = pl.ds(part * LANES, LANES)
-            fine = index_ref[tile, 0, :, lanes] * FRAC + index_ref[tile, 1, :, lanes]
-            cosine, sine = cos_sin((fine * 2861) & 4095)
-            cosine, sine = cosine * scale, sine * scale
-            for s in range(rows):
-                fine_s = spread(fine[s : s + 1])
-                bins_s = fine_s >> 4
-                weight = lane_take(table, ((fine_s & 15) << 3) + ((phase - bins_s) & 7))
-                real_ref[tile, s, part] = weight * spread(cosine[s : s + 1])
-                imag_ref[tile, s, part] = weight * spread(sine[s : s + 1])
-                lane_ref[tile, s, part] = ((bins_s - phase + 7) >> 3) & (LANES - 1)
-    copy.wait()
+    for part in range(length // LANES):
+        lanes = pl.ds(part * LANES, LANES)
+        fine = index_ref[0, :, lanes] * FRAC + index_ref[1, :, lanes]
+        cosine, sine = cos_sin((fine * 2861) & 4095)
+        cosine, sine = cosine * scale, sine * scale
+        for s in range(rows):
+            fine_s = spread(fine[s : s + 1])
+            bins_s = fine_s >> 4
+            weight = lane_take(table, ((fine_s & 15) << 3) + ((phase - bins_s) & 7))
+            real_ref[s, part] = weight * spread(cosine[s : s + 1])
+            imag_ref[s, part] = weight * spread(sine[s : s + 1])
+            lane_ref[s, part] = ((bins_s - phase + 7) >> 3) & (LANES - 1)
+    if before:
+        copy.wait()
 
 
 def row_sums(values):
@@ -123,8 +138,10 @@
     return values[0]
 
 
-def project_kernel(own, first_ref, whole, real_ref, imag_ref, lane_ref, out_ref):
-    tiles, rows, parts = real_ref.shape[:3]
+def project_kernel(own, first_ref, whole, *refs):
+    real_refs, imag_refs, lane_refs, out_ref = refs[0:-1:3], refs[1:-1:3], refs[2:-1:3], refs[-1]
+    tiles = len(real_refs)
+    rows, parts = real_refs[0].shape[:2]
     owners, _, each = whole.shape[:3]
     quarters = rows // each
     halves = BLOCK // LANES
@@ -146,13 +163,13 @@
                     table = [jnp.where(here, whole[owners - 1 - owner, c, p], whole[owners - 1 - after, c, p]) for c in range(2)]
                     for half in range(halves):
                         part = block * halves + half
-                        lane = lane_ref[tile, row, part]
+                        lane = lane_refs[tile][row, part]
                         got = [lane_take(table[c], lane) for c in range(2)]
-                        real, imag = real_ref[tile, row, part], imag_ref[tile, row, part]
+                        real, imag = real_refs[tile][row, part], imag_refs[tile][row, part]
                         total[0][half] = total[0][half] + (got[0] * real - got[1] * imag)
                         total[1][half] = total[1][half] + (got[0] * imag + got[1] * real)
                 sums = total[0] + total[1] + sums
-            out_ref[tiles * quarters - 1 - ((tile ^ near) * quarters + quarter)] = row_sums(sums)
+            out_ref[tiles * quarters - 1 - ((STEPS[tile] ^ near) * quarters + quarter)] = row_sums(sums)
 
 
 def swap(value, step):
@@ -185,33 +202,36 @@
         name="arrange",
     )(*(pltpu.with_memory_space_constraint(value, pltpu.HBM) for value in (profile, base_bin, tap_offset)))
     whole = backward(shards, ("far", "near"))
-    index = jnp.stack([index[0]] + [swap(index[step], step) for step in range(1, SIDE)])
-    by_part = (SIDE, SUBLANES, parts, TAPS, LANES)
-    first, real, imag, lane = pl.pallas_call(
-        lambda *refs: prepare_kernel(scale, *refs),
-        out_shape=[
-            pltpu.SMEM((SUBLANES, LANES), jnp.int32),
-            jax.ShapeDtypeStruct(by_part, jnp.float32),
-            jax.ShapeDtypeStruct(by_part, jnp.float32),
-            jax.ShapeDtypeStruct(by_part, jnp.int32),
-        ],
-        in_specs=[vmem] * 2,
-        out_specs=[smem] + [vmem] * 3,
-        scratch_shapes=[pltpu.VMEM((SUBLANES, LANES), jnp.int32), pltpu.SemaphoreType.DMA],
-        cost_estimate=pl.CostEstimate(flops=pulses * pixels * 300, bytes_accessed=pulses * pixels * 104, transcendentals=0),
-        compiler_params=pltpu.CompilerParams(vmem_limit_bytes=16 << 20),
-        name="prepare",
-    )(tap_table(), index)
+    index = [index[0]] + [swap(index[step], step) for step in STEPS[1:]]
+
+    table = tap_table()
+    prepared, firsts = [], []
+    for tile in range(SIDE):
+        last = tile == SIDE - 1
+        first, *rest = pl.pallas_call(
+            lambda *refs: prepare_kernel(scale, *refs),
+            out_shape=[pltpu.SMEM((SUBLANES, LANES), jnp.int32) if last else jax.ShapeDtypeStruct((SUBLANES, LANES), jnp.int32)]
+            + [jax.ShapeDtypeStruct((SUBLANES, parts, TAPS, LANES), kind) for kind in (jnp.float32, jnp.float32, jnp.int32)],
+            in_specs=[vmem] * (2 + SIDE - 1 if last else 2),
+            out_specs=[smem if last else vmem] + [vmem] * 3,
+            scratch_shapes=[pltpu.VMEM((SUBLANES, LANES), jnp.int32), pltpu.SemaphoreType.DMA] if last else [],
+            cost_estimate=pl.CostEstimate(flops=pulses * pixels * 75, bytes_accessed=pulses * pixels * 26, transcendentals=0),
+            compiler_params=pltpu.CompilerParams(vmem_limit_bytes=16 << 20),
+            name="prepare",
+        )(table, index[tile], *(firsts if last else []))
+        firsts.append(first)
+        prepared += rest
+
     def project(own):
         return pl.pallas_call(
             lambda *refs: project_kernel(own, *refs),
             out_shape=jax.ShapeDtypeStruct((SIDE * quarters, SUBLANES, LANES), jnp.float32),
-            in_specs=[smem] + [vmem] * 4,
+            in_specs=[smem] + [vmem] * (1 + 3 * SIDE),
             out_specs=vmem,
             cost_estimate=pl.CostEstimate(flops=1 << 24, bytes_accessed=2 << 20, transcendentals=0),
             compiler_params=pltpu.CompilerParams(vmem_limit_bytes=24 << 20),
             name="project",
-        )(first, whole, real, imag, lane)
+        )(first, whole, *prepared)
 
     theirs = lax.ppermute(project(False), "core", [(0, 1), (1, 0)])
     partial_image = (project(True) + theirs).reshape(SIDE * pixels // BLOCK // 2, 2 * BLOCK // LANES, LANES)

time: 39.9 us -> 39.2 us (0.982)
  waiting for transfers between devices: 4.71 us -> 3.24 us
  starting transfers between devices: 17.4 us -> 18.1 us
    ppermute x3, waiting for transfers between devices: 4.53 us -> 3.06 us  [swap(): return lax.ppermute(value, 'near', [(i, i ^ step) for i in range(SIDE)])]
    ppermute x1, starting transfers between devices: 0.82 us -> 2.11 us  [local(): theirs = lax.ppermute(project(False), 'core', [(0, 1), (1, 0)])]
    ppermute x3, starting transfers between devices: 3.86 us -> 3.25 us  [swap(): return lax.ppermute(value, 'near', [(i, i ^ step) for i in range(SIDE)])]
    pallas_call x1 -> x4, Pallas kernels: 1.47 us -> 1.64 us  [local(): pl.pallas_call(lambda *refs: prepare_kernel(scale, *refs), out_shape=[plt...]
  transfers between devices with their start and end apart: 5 -> 5, of which waited for: 3 -> 2; matrix products, arithmetic and copies ran while one was open for 1% -> 1% of each run, Pallas kernels for 6% -> 6%
where the time goes in v7:
time: 39.2 us; the launch traced here: 39 us
  starting transfers between devices  18.1 us (46%)
  blocking collectives  11.3 us (29%)
  Pallas kernels  5.09 us (13%)
  waiting for transfers between devices  3.24 us (8%)
  local copies, waits for them, and re-layouts  0.85 us (2%)
    all_to_all x1, starting transfers between devices, backward(): lax.all_to_all(value, axes, 0, 0, tiled=True, axis_index_groups=[list(ran...  12.7 us
    all_to_all x1, blocking collectives, backward(): lax.all_to_all(value, axes, 0, 0, tiled=True, axis_index_groups=[list(ran...  11.3 us
    ppermute x3, starting transfers between devices, swap(): return lax.ppermute(value, 'near', [(i, i ^ step) for i in range(SIDE)])  3.25 us
    ppermute x3, waiting for transfers between devices, swap(): return lax.ppermute(value, 'near', [(i, i ^ step) for i in range(SIDE)])  3.06 us
    ppermute x1, starting transfers between devices, local(): theirs = lax.ppermute(project(False), 'core', [(0, 1), (1, 0)])  2.11 us
    pallas_call x1, Pallas kernels, local(): pl.pallas_call(arrange_kernel, out_shape=[jax.ShapeDtypeStruct((2, SUBLAN...  2.02 us
    pallas_call x4, Pallas kernels, local(): pl.pallas_call(lambda *refs: prepare_kernel(scale, *refs), out_shape=[plt...  1.64 us
    pallas_call x2, Pallas kernels, project(): pl.pallas_call(lambda *refs: project_kernel(own, *refs), out_shape=jax.Sh...  1.43 us
  transfers between devices with their start and end apart: 5, of which 2 were waited for; matrix products, arithmetic and copies ran while one was open for 1% of the time, Pallas kernels for 6%

profile of v7, /device:TPU:1, one launch (start us, length us, event | category | flops | bytes accessed | tf_op | source)
XLA Modules:
  0.0 39.0 jit_solution(14638605638337928194)
XLA Ops:
  0.0 2.0 %arrange.1 = (s32[2,8,1024]{2,1,0:T(8,128)S(1)}, s32[2,8,1024]{2,1,0:T(8,128)S(1)}, s32[2,8,1024]{2,1,0:T(8,128)S(1)}, s32[2,8,1024]{2,1,0:T(8,128)S(1)}, f32[16,2,2,8,128]{4,3,2,1,0:T(8,128)}) custom-call(f32[2,8,1024]{2,1,0:T(8,128)} %shard_ref.1, s32[8,4096]{1,0:T(8,128)} %bins_ref.1, s32[8,4096]{1,0:T(8,128)} %offsets_ref.1), custom_call_target="tpu_custom_call" | custom-call | tf_op jit(solution)/shard_map/arrange/pallas_call | solution.py:194
  2.0 12.7 %all-to-all-start = ((f32[16,2,2,8,128]{4,3,2,1,0:T(8,128)}), f32[16,2,2,8,128]{4,3,2,1,0:T(8,128)S(1)}, u32[]{:S(2)}, u32[]{:S(2)}) async-start(f32[16,2,2,8,128]{4,3,2,1,0:T(8,128)} %get-tuple-element.34), calls=%async_computation | async-start | bytes 524288 | tf_op jit(solution)/shard_map/all_to_all | solution.py:180
  14.7 0.6 %collective-permute-start = (s32[2,8,1024]{2,1,0:T(8,128)S(1)}, s32[2,8,1024]{2,1,0:T(8,128)S(1)}, u32[]{:S(2)}, u32[]{:S(2)}) collective-permute-start(s32[2,8,1024]{2,1,0:T(8,128)S(1)} %get-tuple-element.26), channel_id=1, source_target_pairs={{0,16},{16,0},{32,48},{48,32},{1,17},{17,1},{33,49},{49,33},{2,18}... | collective-permute-start | bytes 196616 | tf_op jit(solution)/shard_map/ppermute | solution.py:176
  15.3 0.9 %collective-permute-start.1 = (s32[2,8,1024]{2,1,0:T(8,128)S(1)}, s32[2,8,1024]{2,1,0:T(8,128)S(1)}, u32[]{:S(2)}, u32[]{:S(2)}) collective-permute-start(s32[2,8,1024]{2,1,0:T(8,128)S(1)} %get-tuple-element.29), channel_id=1, source_target_pairs={{0,48},{16,32},{32,16},{48,0},{1,49},{17,33},{33,17},{49,1},{2,50}... | collective-permute-start | bytes 196616 | tf_op jit(solution)/shard_map/ppermute | solution.py:176
  16.2 1.8 %collective-permute-start.2 = (s32[2,8,1024]{2,1,0:T(8,128)S(1)}, s32[2,8,1024]{2,1,0:T(8,128)S(1)}, u32[]{:S(2)}, u32[]{:S(2)}) collective-permute-start(s32[2,8,1024]{2,1,0:T(8,128)S(1)} %get-tuple-element.31), channel_id=1, source_target_pairs={{0,32},{16,48},{32,0},{48,16},{1,33},{17,49},{33,1},{49,17},{2,34}... | collective-permute-start | bytes 196616 | tf_op jit(solution)/shard_map/ppermute | solution.py:176
  18.0 0.2 broadcast_subtract_fusion
  18.2 0.1 sub.64
  18.3 0.1 div.52
  18.4 0.1 div.53
  18.6 0.3 prepare.4
  18.8 3.1 %collective-permute-done.2.refs_1_ = s32[2,8,1024]{2,1,0:T(8,128)S(1)} collective-permute-done((s32[2,8,1024]{2,1,0:T(8,128)S(1)}, s32[2,8,1024]{2,1,0:T(8,128)S(1)}, u32[]{:S(2)}, u32[]{:S(2)}) %collective-permute-start.2) | collective-permute-done | bytes 65568 | tf_op jit(solution)/shard_map/ppermute | solution.py:176
  21.9 0.3 prepare.6
  22.1 0.0 collective-permute-done.1.refs_1_
  22.1 0.3 prepare.5
  22.4 0.0 collective-permute-done.refs_1_
  22.4 0.8 %prepare.7 = (s32[8,128]{1,0:T(8,128)S(4)}, f32[8,8,8,128]{3,2,1,0:T(8,128)S(1)}, f32[8,8,8,128]{3,2,1,0:T(8,128)S(1)}, s32[8,8,8,128]{3,2,1,0:T(8,128)S(1)}) custom-call(f32[1,128]{1,0:T(1,128)S(1)} %fusion.30.refs_0_, s32[2,8,1024]{2,1,0:T(8,128)S(1)} %collective-permute-done.refs_1_, s32[8,128]{1,0:T(8,128)S(1)} %get-tuple-element.28.refs_2_, ...), custom_call_target="tpu_custom_call" | custom-call | flops 2457600 | bytes 851968 | tf_op jit(solution)/shard_map/prepare/pallas_call | solution.py:211
  23.3 0.0 all-to-all-done.refs_1_
  23.3 0.7 %project.3 = f32[16,8,128]{2,1,0:T(8,128)S(1)} custom-call(s32[8,128]{1,0:T(8,128)S(4)} %get-tuple-element.33.refs_0_, f32[16,2,2,8,128]{4,3,2,1,0:T(8,128)S(1)} %all-to-all-done.refs_1_, f32[8,8,8,128]{3,2,1,0:T(8,128)S(1)} %get-tuple-element.35.refs_2_, f32[8,8,8,128]{3,2,1,0:T(8,128)S(1)} %get-tuple-element.36.refs_3_, ...), custom_call_target="tpu_custom_call" | custom-call | flops 16777216 | bytes 2097152 | tf_op jit(solution)/shard_map/project/pallas_call | solution.py:226
  24.0 2.1 %collective-permute-start.3 = (f32[16,8,128]{2,1,0:T(8,128)S(1)}, f32[16,8,128]{2,1,0:T(8,128)S(1)}, u32[]{:S(2)}, u32[]{:S(2)}) collective-permute-start(f32[16,8,128]{2,1,0:T(8,128)S(1)} %project.3), channel_id=1, source_target_pairs={{0,1},{1,0},{2,3},{3,2},{4,5},{5,4},{6,7},{7,6},{8,9},{9,8},{10,11... | collective-permute-start | bytes 196616 | tf_op jit(solution)/shard_map/ppermute | solution.py:236
  26.1 0.7 %project.2 = f32[16,8,128]{2,1,0:T(8,128)S(1)} custom-call(s32[8,128]{1,0:T(8,128)S(4)} %get-tuple-element.33.refs_0_, f32[16,2,2,8,128]{4,3,2,1,0:T(8,128)S(1)} %all-to-all-done.refs_1_, f32[8,8,8,128]{3,2,1,0:T(8,128)S(1)} %get-tuple-element.35.refs_2_, f32[8,8,8,128]{3,2,1,0:T(8,128)S(1)} %get-tuple-element.36.refs_3_, ...), custom_call_target="tpu_custom_call" | custom-call | flops 16777216 | bytes 2097152 | tf_op jit(solution)/shard_map/project/pallas_call | solution.py:226
  26.8 0.2 collective-permute-done.3
  27.0 11.3 %all_to_all.10 = f32[32,4,128]{2,1,0:T(4,128)S(1)} all-to-all(f32[32,4,128]{2,1,0:T(4,128)S(1)} %bitcast.1), channel_id=1, replica_groups={{62,60,58,56,54,52,50,48,46,44,42,40,38,36,34,32,30,28,26,24,22,20,18,1..., dimensions={0} | all-to-all | bytes 131072 | tf_op jit(solution)/shard_map/all_to_all | solution.py:180
  38.4 0.6 %reshape.167 = f32[2,256]{1,0:T(2,128)} reshape(f32[4,128]{1,0:T(4,128)S(1)} %reduce_sum.19) | data formatting | bytes 4096 | tf_op jit(solution)/shard_map/reshape | solution.py:239
  (5 shorter events, 0.1 us)
Async XLA Ops:
  2.0 21.2 %all-to-all-start = ((f32[16,2,2,8,128]{4,3,2,1,0:T(8,128)}), f32[16,2,2,8,128]{4,3,2,1,0:T(8,128)S(1)}, u32[]{:S(2)}, u32[]{:S(2)}) async-start(f32[16,2,2,8,128]{4,3,2,1,0:T(8,128)} %get-tuple-element.34), calls=%async_computation | async-start | bytes 524288 | tf_op jit(solution)/shard_map/all_to_all | solution.py:180
  14.7 7.7 %collective-permute-start = (s32[2,8,1024]{2,1,0:T(8,128)S(1)}, s32[2,8,1024]{2,1,0:T(8,128)S(1)}, u32[]{:S(2)}, u32[]{:S(2)}) collective-permute-start(s32[2,8,1024]{2,1,0:T(8,128)S(1)} %get-tuple-element.26), channel_id=1, source_target_pairs={{0,16},{16,0},{32,48},{48,32},{1,17},{17,1},{33,49},{49,33},{2,18}... | collective-permute-start | bytes 196616 | tf_op jit(solution)/shard_map/ppermute | solution.py:176
  15.3 6.8 %collective-permute-start.1 = (s32[2,8,1024]{2,1,0:T(8,128)S(1)}, s32[2,8,1024]{2,1,0:T(8,128)S(1)}, u32[]{:S(2)}, u32[]{:S(2)}) collective-permute-start(s32[2,8,1024]{2,1,0:T(8,128)S(1)} %get-tuple-element.29), channel_id=1, source_target_pairs={{0,48},{16,32},{32,16},{48,0},{1,49},{17,33},{33,17},{49,1},{2,50}... | collective-permute-start | bytes 196616 | tf_op jit(solution)/shard_map/ppermute | solution.py:176
  16.2 5.7 %collective-permute-start.2 = (s32[2,8,1024]{2,1,0:T(8,128)S(1)}, s32[2,8,1024]{2,1,0:T(8,128)S(1)}, u32[]{:S(2)}, u32[]{:S(2)}) collective-permute-start(s32[2,8,1024]{2,1,0:T(8,128)S(1)} %get-tuple-element.31), channel_id=1, source_target_pairs={{0,32},{16,48},{32,0},{48,16},{1,33},{17,49},{33,1},{49,17},{2,34}... | collective-permute-start | bytes 196616 | tf_op jit(solution)/shard_map/ppermute | solution.py:176
  24.0 3.0 %collective-permute-start.3 = (f32[16,8,128]{2,1,0:T(8,128)S(1)}, f32[16,8,128]{2,1,0:T(8,128)S(1)}, u32[]{:S(2)}, u32[]{:S(2)}) collective-permute-start(f32[16,8,128]{2,1,0:T(8,128)S(1)} %project.3), channel_id=1, source_target_pairs={{0,1},{1,0},{2,3},{3,2},{4,5},{5,4},{6,7},{7,6},{8,9},{9,8},{10,11... | collective-permute-start | bytes 196616 | tf_op jit(solution)/shard_map/ppermute | solution.py:236

commit v8 on v7

--- a/solution.py
+++ b/solution.py
@@ -15,6 +15,7 @@
 SUBLANES = 8
 SIDE = 4
 STEPS = (0, 3, 2, 1)
+START = 20
 AXES = ("far", "near", "x", "pair", "core")
 SIZES = (4, 4, 4, 2, 2)
 
@@ -168,8 +169,8 @@
                         real, imag = real_refs[tile][row, part], imag_refs[tile][row, part]
                         total[0][half] = total[0][half] + (got[0] * real - got[1] * imag)
                         total[1][half] = total[1][half] + (got[0] * imag + got[1] * real)
-                sums = total[0] + total[1] + sums
-            out_ref[tiles * quarters - 1 - ((STEPS[tile] ^ near) * quarters + quarter)] = row_sums(sums)
+                sums = sums + total[0] + total[1]
+            out_ref[((STEPS[tile] ^ near) * quarters + quarter - START // 2) & (tiles * quarters - 1)] = row_sums(sums)
 
 
 def swap(value, step):
@@ -235,7 +236,9 @@
 
     theirs = lax.ppermute(project(False), "core", [(0, 1), (1, 0)])
     partial_image = (project(True) + theirs).reshape(SIDE * pixels // BLOCK // 2, 2 * BLOCK // LANES, LANES)
-    received = backward(partial_image, ("near", "x", "pair"))
+    count = partial_image.shape[0]
+    order = [(START + i) % count for i in range(count)]
+    received = lax.all_to_all(partial_image, ("near", "x", "pair"), 0, 0, tiled=True, axis_index_groups=[order])
     return jnp.sum(received, axis=0).reshape(2, BLOCK)
 
 

time: 39.2 us -> 38.7 us (0.987)
  blocking collectives: 11.3 us -> 10.8 us
    all_to_all x1, blocking collectives: 11.3 us -> 10.8 us  [local(): lax.all_to_all(partial_image, ('near', 'x', 'pair'), 0, 0, tiled=True, ax...]
where the time goes in v8:
time: 38.7 us; the launch traced here: 38.4 us
  starting transfers between devices  18.1 us (47%)
  blocking collectives  10.8 us (28%)
  Pallas kernels  5.09 us (13%)
  waiting for transfers between devices  3.24 us (8%)
  local copies, waits for them, and re-layouts  0.85 us (2%)
    all_to_all x1, starting transfers between devices, backward(): lax.all_to_all(value, axes, 0, 0, tiled=True, axis_index_groups=[list(ran...  12.7 us
    all_to_all x1, blocking collectives, local(): lax.all_to_all(partial_image, ('near', 'x', 'pair'), 0, 0, tiled=True, ax...  10.8 us
    ppermute x3, starting transfers between devices, swap(): return lax.ppermute(value, 'near', [(i, i ^ step) for i in range(SIDE)])  3.25 us
    ppermute x3, waiting for transfers between devices, swap(): return lax.ppermute(value, 'near', [(i, i ^ step) for i in range(SIDE)])  3.06 us
    ppermute x1, starting transfers between devices, local(): theirs = lax.ppermute(project(False), 'core', [(0, 1), (1, 0)])  2.11 us
    pallas_call x1, Pallas kernels, local(): pl.pallas_call(arrange_kernel, out_shape=[jax.ShapeDtypeStruct((2, SUBLAN...  2.02 us
    pallas_call x4, Pallas kernels, local(): pl.pallas_call(lambda *refs: prepare_kernel(scale, *refs), out_shape=[plt...  1.64 us
    pallas_call x2, Pallas kernels, project(): pl.pallas_call(lambda *refs: project_kernel(own, *refs), out_shape=jax.Sh...  1.43 us
  transfers between devices with their start and end apart: 5, of which 2 were waited for; matrix products, arithmetic and copies ran while one was open for 1% of the time, Pallas kernels for 6%

profile of v8, /device:TPU:1, one launch (start us, length us, event | category | flops | bytes accessed | tf_op | source)
XLA Modules:
  0.0 38.4 jit_solution(16774817472369716036)
XLA Ops:
  0.0 2.0 %arrange.1 = (s32[2,8,1024]{2,1,0:T(8,128)S(1)}, s32[2,8,1024]{2,1,0:T(8,128)S(1)}, s32[2,8,1024]{2,1,0:T(8,128)S(1)}, s32[2,8,1024]{2,1,0:T(8,128)S(1)}, f32[16,2,2,8,128]{4,3,2,1,0:T(8,128)}) custom-call(f32[2,8,1024]{2,1,0:T(8,128)} %shard_ref.1, s32[8,4096]{1,0:T(8,128)} %bins_ref.1, s32[8,4096]{1,0:T(8,128)} %offsets_ref.1), custom_call_target="tpu_custom_call" | custom-call | tf_op jit(solution)/shard_map/arrange/pallas_call | solution.py:195
  2.0 12.7 %all-to-all-start = ((f32[16,2,2,8,128]{4,3,2,1,0:T(8,128)}), f32[16,2,2,8,128]{4,3,2,1,0:T(8,128)S(1)}, u32[]{:S(2)}, u32[]{:S(2)}) async-start(f32[16,2,2,8,128]{4,3,2,1,0:T(8,128)} %get-tuple-element.34), calls=%async_computation | async-start | bytes 524288 | tf_op jit(solution)/shard_map/all_to_all | solution.py:181
  14.7 0.6 %collective-permute-start = (s32[2,8,1024]{2,1,0:T(8,128)S(1)}, s32[2,8,1024]{2,1,0:T(8,128)S(1)}, u32[]{:S(2)}, u32[]{:S(2)}) collective-permute-start(s32[2,8,1024]{2,1,0:T(8,128)S(1)} %get-tuple-element.26), channel_id=1, source_target_pairs={{0,16},{16,0},{32,48},{48,32},{1,17},{17,1},{33,49},{49,33},{2,18}... | collective-permute-start | bytes 196616 | tf_op jit(solution)/shard_map/ppermute | solution.py:177
  15.3 0.9 %collective-permute-start.1 = (s32[2,8,1024]{2,1,0:T(8,128)S(1)}, s32[2,8,1024]{2,1,0:T(8,128)S(1)}, u32[]{:S(2)}, u32[]{:S(2)}) collective-permute-start(s32[2,8,1024]{2,1,0:T(8,128)S(1)} %get-tuple-element.29), channel_id=1, source_target_pairs={{0,48},{16,32},{32,16},{48,0},{1,49},{17,33},{33,17},{49,1},{2,50}... | collective-permute-start | bytes 196616 | tf_op jit(solution)/shard_map/ppermute | solution.py:177
  16.2 1.8 %collective-permute-start.2 = (s32[2,8,1024]{2,1,0:T(8,128)S(1)}, s32[2,8,1024]{2,1,0:T(8,128)S(1)}, u32[]{:S(2)}, u32[]{:S(2)}) collective-permute-start(s32[2,8,1024]{2,1,0:T(8,128)S(1)} %get-tuple-element.31), channel_id=1, source_target_pairs={{0,32},{16,48},{32,0},{48,16},{1,33},{17,49},{33,1},{49,17},{2,34}... | collective-permute-start | bytes 196616 | tf_op jit(solution)/shard_map/ppermute | solution.py:177
  18.0 0.2 broadcast_subtract_fusion
  18.2 0.1 sub.64
  18.3 0.1 div.52
  18.4 0.1 div.53
  18.6 0.3 prepare.4
  18.8 3.1 %collective-permute-done.2.refs_1_ = s32[2,8,1024]{2,1,0:T(8,128)S(1)} collective-permute-done((s32[2,8,1024]{2,1,0:T(8,128)S(1)}, s32[2,8,1024]{2,1,0:T(8,128)S(1)}, u32[]{:S(2)}, u32[]{:S(2)}) %collective-permute-start.2) | collective-permute-done | bytes 65568 | tf_op jit(solution)/shard_map/ppermute | solution.py:177
  21.9 0.3 prepare.6
  22.1 0.0 collective-permute-done.1.refs_1_
  22.1 0.3 prepare.5
  22.4 0.0 collective-permute-done.refs_1_
  22.4 0.8 %prepare.7 = (s32[8,128]{1,0:T(8,128)S(4)}, f32[8,8,8,128]{3,2,1,0:T(8,128)S(1)}, f32[8,8,8,128]{3,2,1,0:T(8,128)S(1)}, s32[8,8,8,128]{3,2,1,0:T(8,128)S(1)}) custom-call(f32[1,128]{1,0:T(1,128)S(1)} %fusion.30.refs_0_, s32[2,8,1024]{2,1,0:T(8,128)S(1)} %collective-permute-done.refs_1_, s32[8,128]{1,0:T(8,128)S(1)} %get-tuple-element.28.refs_2_, ...), custom_call_target="tpu_custom_call" | custom-call | flops 2457600 | bytes 851968 | tf_op jit(solution)/shard_map/prepare/pallas_call | solution.py:212
  23.3 0.0 all-to-all-done.refs_1_
  23.3 0.7 %project.3 = f32[16,8,128]{2,1,0:T(8,128)S(1)} custom-call(s32[8,128]{1,0:T(8,128)S(4)} %get-tuple-element.33.refs_0_, f32[16,2,2,8,128]{4,3,2,1,0:T(8,128)S(1)} %all-to-all-done.refs_1_, f32[8,8,8,128]{3,2,1,0:T(8,128)S(1)} %get-tuple-element.35.refs_2_, f32[8,8,8,128]{3,2,1,0:T(8,128)S(1)} %get-tuple-element.36.refs_3_, ...), custom_call_target="tpu_custom_call" | custom-call | flops 16777216 | bytes 2097152 | tf_op jit(solution)/shard_map/project/pallas_call | solution.py:227
  24.0 2.1 %collective-permute-start.3 = (f32[16,8,128]{2,1,0:T(8,128)S(1)}, f32[16,8,128]{2,1,0:T(8,128)S(1)}, u32[]{:S(2)}, u32[]{:S(2)}) collective-permute-start(f32[16,8,128]{2,1,0:T(8,128)S(1)} %project.3), channel_id=1, source_target_pairs={{0,1},{1,0},{2,3},{3,2},{4,5},{5,4},{6,7},{7,6},{8,9},{9,8},{10,11... | collective-permute-start | bytes 196616 | tf_op jit(solution)/shard_map/ppermute | solution.py:237
  26.1 0.7 %project.2 = f32[16,8,128]{2,1,0:T(8,128)S(1)} custom-call(s32[8,128]{1,0:T(8,128)S(4)} %get-tuple-element.33.refs_0_, f32[16,2,2,8,128]{4,3,2,1,0:T(8,128)S(1)} %all-to-all-done.refs_1_, f32[8,8,8,128]{3,2,1,0:T(8,128)S(1)} %get-tuple-element.35.refs_2_, f32[8,8,8,128]{3,2,1,0:T(8,128)S(1)} %get-tuple-element.36.refs_3_, ...), custom_call_target="tpu_custom_call" | custom-call | flops 16777216 | bytes 2097152 | tf_op jit(solution)/shard_map/project/pallas_call | solution.py:227
  26.8 0.2 collective-permute-done.3
  27.0 10.8 %all_to_all.10 = f32[32,4,128]{2,1,0:T(4,128)S(1)} all-to-all(f32[32,4,128]{2,1,0:T(4,128)S(1)} %bitcast.1), channel_id=1, replica_groups={{40,42,44,46,48,50,52,54,56,58,60,62,0,2,4,6,8,10,12,14,16,18,20,22,24,..., dimensions={0} | all-to-all | bytes 131072 | tf_op jit(solution)/shard_map/all_to_all | solution.py:241
  37.8 0.6 %reshape.167 = f32[2,256]{1,0:T(2,128)} reshape(f32[4,128]{1,0:T(4,128)S(1)} %reduce_sum.19) | data formatting | bytes 4096 | tf_op jit(solution)/shard_map/reshape | solution.py:242
  (5 shorter events, 0.1 us)
Async XLA Ops:
  2.0 21.2 %all-to-all-start = ((f32[16,2,2,8,128]{4,3,2,1,0:T(8,128)}), f32[16,2,2,8,128]{4,3,2,1,0:T(8,128)S(1)}, u32[]{:S(2)}, u32[]{:S(2)}) async-start(f32[16,2,2,8,128]{4,3,2,1,0:T(8,128)} %get-tuple-element.34), calls=%async_computation | async-start | bytes 524288 | tf_op jit(solution)/shard_map/all_to_all | solution.py:181
  14.7 7.7 %collective-permute-start = (s32[2,8,1024]{2,1,0:T(8,128)S(1)}, s32[2,8,1024]{2,1,0:T(8,128)S(1)}, u32[]{:S(2)}, u32[]{:S(2)}) collective-permute-start(s32[2,8,1024]{2,1,0:T(8,128)S(1)} %get-tuple-element.26), channel_id=1, source_target_pairs={{0,16},{16,0},{32,48},{48,32},{1,17},{17,1},{33,49},{49,33},{2,18}... | collective-permute-start | bytes 196616 | tf_op jit(solution)/shard_map/ppermute | solution.py:177
  15.3 6.8 %collective-permute-start.1 = (s32[2,8,1024]{2,1,0:T(8,128)S(1)}, s32[2,8,1024]{2,1,0:T(8,128)S(1)}, u32[]{:S(2)}, u32[]{:S(2)}) collective-permute-start(s32[2,8,1024]{2,1,0:T(8,128)S(1)} %get-tuple-element.29), channel_id=1, source_target_pairs={{0,48},{16,32},{32,16},{48,0},{1,49},{17,33},{33,17},{49,1},{2,50}... | collective-permute-start | bytes 196616 | tf_op jit(solution)/shard_map/ppermute | solution.py:177
  16.2 5.7 %collective-permute-start.2 = (s32[2,8,1024]{2,1,0:T(8,128)S(1)}, s32[2,8,1024]{2,1,0:T(8,128)S(1)}, u32[]{:S(2)}, u32[]{:S(2)}) collective-permute-start(s32[2,8,1024]{2,1,0:T(8,128)S(1)} %get-tuple-element.31), channel_id=1, source_target_pairs={{0,32},{16,48},{32,0},{48,16},{1,33},{17,49},{33,1},{49,17},{2,34}... | collective-permute-start | bytes 196616 | tf_op jit(solution)/shard_map/ppermute | solution.py:177
  24.0 3.0 %collective-permute-start.3 = (f32[16,8,128]{2,1,0:T(8,128)S(1)}, f32[16,8,128]{2,1,0:T(8,128)S(1)}, u32[]{:S(2)}, u32[]{:S(2)}) collective-permute-start(f32[16,8,128]{2,1,0:T(8,128)S(1)} %project.3), channel_id=1, source_target_pairs={{0,1},{1,0},{2,3},{3,2},{4,5},{5,4},{6,7},{7,6},{8,9},{9,8},{10,11... | collective-permute-start | bytes 196616 | tf_op jit(solution)/shard_map/ppermute | solution.py:237
